TPU v7x, 256 devices: a whole 4x4x8 slice. The times are simulated.
256 devices in a mesh: dp: 16 (over z, y_lo), cp: 16 (over x, y_hi, core).
Axes of the slice: x: 4, y: 4 (y_hi: 2, y_lo: 2; y = y_hi * 2 + y_lo), z: 8, core: 2. Of those that a mesh axis runs over, the one named last changes fastest.
Arguments:
- layer_input: bfloat16 [32768, 4096], P(('dp', 'cp')), may hold values from -0.75 to 0.75
- queries: bfloat16 [32768, 2048], P(('dp', 'cp')), may hold values from -6 to 6
- keys: bfloat16 [32768, 512], P(('dp', 'cp')), may hold values from -6 to 6
- values: bfloat16 [32768, 512], P(('dp', 'cp')), may hold values from -6 to 6
- outputs: bfloat16 [32768, 2048], P(('dp', 'cp')), may hold values from -6 to 6
- out_grad: bfloat16 [32768, 2048], P(('dp', 'cp')), may hold values from -1.5 to 1.5
- log_sum_exp: float32 [32768, 16], P(('dp', 'cp')), may hold values from 5 to 8
- group_first: int32 [16, 16], P('dp', 'cp'), may hold values from 0 to 12, as said below
- span_index: int32 [16, 16], P('dp', 'cp'), may hold values from 0 to 15, as said below
- seq_length: int32 [16, 16], P('dp', 'cp'), may hold values from 1 to 2048, as said below
Outputs:
- query_grad: bfloat16 [32768, 2048], P(('dp', 'cp'))
- weight_grad: bfloat16 [4096, 1024], P(('dp', 'cp'))
Inputs may be any that keep to these rules, and one draw needn't show every extreme that they name: Each plan row cuts its 16 members into one to four contiguous groups, each beginning at a member whose index is a multiple of 4; group_first holds the first member of each member's group. Row 0 is always one group of all 16 members; in the last row the last 4 members always form a group of their own. `span_index`: within each group the span indices are a permutation of 0 to the group's size minus 1. `seq_length`: equal for all members of a group; for a group of m members it lies between (m - 1) * 128 + 1 and m * 128. Row 0's is 2048.
All inputs are finite; a program needn't handle non-finite values.
Results may differ from a plain program's by a relative error of at most 0.0062.
Values may be sent and summed in bfloat16 or wider, within the bound.
A program may use at most 128 MiB of HBM per device.

v0:
```python
import jax
import jax.numpy as jnp
from jax import lax
from jax.sharding import PartitionSpec as P

DH = 128


rope_base = 500000.0


def shifted(value, axis, steps):
    count = lax.axis_size(axis)
    pairs = [(source, (source + steps) % count) for source in range(count)]
    return lax.ppermute(value, axis, pairs)


def rope_back(grads, positions):
    half = DH // 2
    freq = rope_base ** (-(jnp.arange(half).astype(jnp.float32) * 2.0 / DH))
    angles = positions.astype(jnp.float32)[:, None] * freq[None, :]
    cosine = jnp.cos(angles)[:, None, :]
    sine = jnp.sin(angles)[:, None, :]
    lower = grads[..., :half]
    upper = grads[..., half:]
    return jnp.concatenate([lower * cosine + upper * sine, upper * cosine - lower * sine], axis=-1)


def shards(
    layer_input,
    queries,
    keys,
    values,
    outputs,
    out_grad,
    log_sum_exp,
    group_first,
    span_index,
    seq_length,
):
    rows_here = layer_input.shape[0]
    kv_heads = keys.shape[1] // DH
    group_width = queries.shape[1] // keys.shape[1]
    kv_cols = kv_heads * DH
    scale_factor = 1.0 / DH**0.5
    query_heads = queries.reshape(rows_here, kv_heads, group_width, DH)
    grad_heads = out_grad.reshape(rows_here, kv_heads, group_width, DH)
    saved_heads = outputs.reshape(rows_here, kv_heads, group_width, DH)
    row_delta = jnp.sum(
        grad_heads.astype(jnp.float32) * saved_heads.astype(jnp.float32), axis=-1
    ).transpose(1, 2, 0)
    lse_heads = log_sum_exp.reshape(rows_here, kv_heads, group_width).transpose(1, 2, 0)
    my_first = group_first[0, 0]
    my_span = span_index[0, 0]
    my_length = seq_length[0, 0]
    offsets = jnp.arange(rows_here, dtype=jnp.int32)
    query_pos = my_span * rows_here + offsets
    plan_tags = jnp.concatenate([group_first, span_index], axis=1)
    key_value = jnp.concatenate([keys, values], axis=1)

    def grad_tables(key_block, value_block, allowed):
        attn_scores = (
            jnp.einsum("qhgd,khd->hgqk", query_heads, key_block, preferred_element_type=jnp.float32)
            * scale_factor
        )
        attn_probs = jnp.exp(
            jnp.where(allowed[None, None], attn_scores - lse_heads[..., None], -jnp.inf)
        )
        grad_probs = jnp.einsum(
            "qhgd,khd->hgqk", grad_heads, value_block, preferred_element_type=jnp.float32
        )
        scores_low = (attn_probs * (grad_probs - row_delta[..., None])).astype(jnp.bfloat16)
        return (attn_probs.astype(jnp.bfloat16), scores_low)

    def kv_terms(probs_low, scores_low):
        key_grad = (
            jnp.einsum(
                "hgqk,qhgd->khd", scores_low, query_heads, preferred_element_type=jnp.float32
            )
            * scale_factor
        )
        value_grad = jnp.einsum(
            "hgqk,qhgd->khd", probs_low, grad_heads, preferred_element_type=jnp.float32
        )
        width_rows = key_grad.shape[0]
        return jnp.concatenate(
            [key_grad.reshape(width_rows, kv_cols), value_grad.reshape(width_rows, kv_cols)], axis=1
        )

    def block_grads(block_kv, source_first, source_span):
        key_block = block_kv[:, :kv_cols].reshape(rows_here, kv_heads, DH)
        value_block = block_kv[:, kv_cols:].reshape(rows_here, kv_heads, DH)
        key_pos = source_span * rows_here + offsets
        allowed = (
            (source_first == my_first)
            & (key_pos[None, :] <= query_pos[:, None])
            & (query_pos[:, None] < my_length)
        )
        probs_low, scores_low = grad_tables(key_block, value_block, allowed)
        query_part = (
            jnp.einsum("hgqk,khd->qhgd", scores_low, key_block, preferred_element_type=jnp.float32)
            * scale_factor
        )
        return (query_part, kv_terms(probs_low, scores_low))

    zero_query = jnp.zeros((rows_here, kv_heads, group_width, DH), jnp.float32)
    zero_kv = jnp.zeros((rows_here, 2 * kv_cols), jnp.float32)

    def maybe_block(block_kv, source_tags):
        source_first = source_tags[0, 0]
        source_span = source_tags[0, 1]
        active = (
            (source_first == my_first)
            & (source_span <= my_span)
            & (my_span * rows_here < my_length)
        )
        return lax.cond(
            active,
            lambda: block_grads(block_kv, source_first, source_span),
            lambda: (zero_query, zero_kv),
        )

    query_start, kv_start = maybe_block(key_value, plan_tags)

    def cycle_turn(turn_index, carried):
        block_kv, block_tags, kv_acc, query_acc = carried
        block_kv, block_tags = shifted((block_kv, block_tags), "cp", 1)
        kv_acc = shifted(kv_acc, "cp", 1)
        query_part, kv_part = maybe_block(block_kv, block_tags)
        return (block_kv, block_tags, kv_acc + kv_part, query_acc + query_part)

    finished = lax.fori_loop(
        1, lax.axis_size("cp"), cycle_turn, (key_value, plan_tags, kv_start, query_start)
    )
    query_grad = finished[3]
    kv_grad = shifted(finished[2], "cp", 1)
    key_plain = rope_back(kv_grad[:, :kv_cols].reshape(rows_here, kv_heads, DH), query_pos)
    kv_stack = jnp.concatenate(
        [key_plain.reshape(rows_here, kv_cols), kv_grad[:, kv_cols:]], axis=1
    ).astype(jnp.bfloat16)
    weight_grad = lax.psum_scatter(
        lax.dot_general(
            layer_input, kv_stack, (((0,), (0,)), ((), ())), preferred_element_type=jnp.float32
        ),
        ("dp", "cp"),
        scatter_dimension=0,
        tiled=True,
    )
    return (
        query_grad.reshape(rows_here, queries.shape[1]).astype(jnp.bfloat16),
        weight_grad.astype(jnp.bfloat16),
    )


def solution(mesh):
    placed = (
        P(("dp", "cp"), None),
        P(("dp", "cp"), None),
        P(("dp", "cp"), None),
        P(("dp", "cp"), None),
        P(("dp", "cp"), None),
        P(("dp", "cp"), None),
        P(("dp", "cp"), None),
        P("dp", "cp"),
        P("dp", "cp"),
        P("dp", "cp"),
    )
    return jax.shard_map(
        shards,
        mesh=mesh,
        in_specs=placed,
        out_specs=(P(("dp", "cp"), None), P(("dp", "cp"), None)),
        check_vma=False,
    )
```

profile of v0, /device:TPU:1, one launch (start us, length us, event | category | flops | bytes accessed | tf_op | source)
XLA Modules:
  0.0 1779.4 jit_solution(18437908421256177802)
XLA Ops:
  16.2 7.5 conditional.2
  23.6 405.0 %while.19 = (s32[]{:T(128)}, bf16[128,1024]{0,1:T(8,128)(2,1)}, s32[1,2]{1,0:T(1,128)S(1)}, f32[128,1024]{0,1:T(8,128)}, f32[128,4,4,128]{3,0,2,1:T(8,128)}, /*i...) while((s32[]{:T(128)}, bf16[128,1024]{0,1:T(8,128)(2,1)}, ...), condition=%wide.region_6.7_spmd.clone, body=%wide.region_3.6_spmd.clone.sunk | while | flops 338280832 | bytes 18796788 | solution.py:132
  23.6 4.3 collective-permute-start.2
  29.3 7.9 collective-permute-done.1
  40.3 5.9 conditional.5
  46.1 2.4 add.82
  49.2 2.0 add.81
  51.3 6.2 collective-permute-start.1
  57.5 3.0 collective-permute-done.1
  64.6 2.4 add.82
  69.7 3.9 collective-permute-start.2
  73.7 2.3 collective-permute-start
  75.9 9.8 collective-permute-start.1
  89.5 5.9 conditional.5
  95.4 2.4 add.82
  100.5 3.6 collective-permute-start
  104.1 4.8 collective-permute-start.1
  113.9 5.9 conditional.5
  119.8 2.4 add.82
  124.9 2.9 collective-permute-start.2
  127.8 4.4 collective-permute-start.1
  132.2 8.0 collective-permute-done.1
  143.3 5.9 conditional.5
  149.2 2.4 add.82
  155.5 9.2 collective-permute-done.1
  168.8 2.4 add.82
  173.9 3.6 collective-permute-start.2
  178.9 4.8 collective-permute-start.1
  183.7 10.4 collective-permute-done.1
  197.2 5.9 conditional.5
  203.1 2.4 add.82
  208.2 3.7 collective-permute-start.1
  211.9 6.7 collective-permute-done.1
  222.6 2.4 add.82
  227.8 7.7 collective-permute-start.2
  235.6 4.5 collective-permute-start.1
  240.1 4.7 collective-permute-done.1
  247.8 5.9 conditional.5
  253.7 2.4 add.82
  258.9 4.6 collective-permute-start
  263.5 4.7 collective-permute-done.1
  272.2 2.4 add.82
  277.3 3.9 collective-permute-start.2
  281.9 9.8 collective-permute-start.1
  291.6 5.3 collective-permute-done.1
  300.0 5.9 conditional.5
  305.9 2.4 add.82
  311.1 3.8 collective-permute-start.1
  314.9 11.5 collective-permute-done.1
  329.4 5.9 conditional.5
  335.3 2.4 add.82
  340.5 15.3 collective-permute-done.1
  358.8 5.9 conditional.5
  364.7 2.4 add.82
  369.9 15.3 collective-permute-done.1
  388.2 5.9 conditional.5
  394.1 2.4 add.82
  399.3 15.3 collective-permute-done.1
  417.6 5.9 conditional.5
  423.5 2.4 add.82
  428.9 11.1 collective-permute-done.3
  440.1 8.1 convolution_bitcast_fusion.4
  448.1 17.4 copy.108
  468.5 1302.3 %reduce-scatter.4.cloned.1.call-done = f32[16,1024]{1,0:T(8,128)} async-done(((f32[4096,1024]{1,0:T(8,128)}), f32[16,1024]{1,0:T(8,128)}) %reduce-scatter.4.cloned.1.call-update) | async-done | bytes 65552
  (293 shorter events, 125.4 us)
Async XLA Ops:
  7.2 432.9 %copy-start = (bf16[128,4096]{1,0:T(8,128)(2,1)S(1)}, bf16[128,4096]{1,0:T(8,128)(2,1)}, u32[]{:S(2)}) copy-start(bf16[128,4096]{1,0:T(8,128)(2,1)} %param.16) | copy-start | bytes 3145732
  7.2 1763.7 %reduce-scatter.4.cloned.1.call-start = ((), (), s32[]{:S(2)}) async-start(), calls=%async_computation.1 | async-start | bytes 16842752
  23.6 25.6 %collective-permute-start.2 = (f32[128,1024]{0,1:T(8,128)}, f32[128,1024]{0,1:T(8,128)}, u32[]{:S(2)}, u32[]{:S(2)}) collective-permute-start(f32[128,1024]{0,1:T(8,128)} %get-tuple-element.464), channel_id=1, source_target_pairs={{0,1},{1,2},{2,3},{3,4},{4,5},{5,6},{6,7},{7,8},{8,9},{9,10},{10,1... | collective-permute-start | bytes 1572872 | tf_op jit(solution)/shard_map/while/body/eval_jaxpr/ppermute | solution.py:15
  27.9 12.3 collective-permute-start
  28.0 9.2 collective-permute-start.1
  51.3 16.4 collective-permute-start.2
  51.3 12.3 collective-permute-start
  51.3 9.2 collective-permute-start.1
  69.7 28.8 %collective-permute-start.2 = (f32[128,1024]{0,1:T(8,128)}, f32[128,1024]{0,1:T(8,128)}, u32[]{:S(2)}, u32[]{:S(2)}) collective-permute-start(f32[128,1024]{0,1:T(8,128)} %get-tuple-element.464), channel_id=1, source_target_pairs={{0,1},{1,2},{2,3},{3,4},{4,5},{5,6},{6,7},{7,8},{8,9},{9,10},{10,1... | collective-permute-start | bytes 1572872 | tf_op jit(solution)/shard_map/while/body/eval_jaxpr/ppermute | solution.py:15
  73.7 15.8 collective-permute-start
  75.9 10.5 collective-permute-start.1
  100.5 22.4 %collective-permute-start.2 = (f32[128,1024]{0,1:T(8,128)}, f32[128,1024]{0,1:T(8,128)}, u32[]{:S(2)}, u32[]{:S(2)}) collective-permute-start(f32[128,1024]{0,1:T(8,128)} %get-tuple-element.464), channel_id=1, source_target_pairs={{0,1},{1,2},{2,3},{3,4},{4,5},{5,6},{6,7},{7,8},{8,9},{9,10},{10,1... | collective-permute-start | bytes 1572872 | tf_op jit(solution)/shard_map/while/body/eval_jaxpr/ppermute | solution.py:15
  100.5 13.4 collective-permute-start
  104.1 6.7 collective-permute-start.1
  124.9 27.4 %collective-permute-start.2 = (f32[128,1024]{0,1:T(8,128)}, f32[128,1024]{0,1:T(8,128)}, u32[]{:S(2)}, u32[]{:S(2)}) collective-permute-start(f32[128,1024]{0,1:T(8,128)} %get-tuple-element.464), channel_id=1, source_target_pairs={{0,1},{1,2},{2,3},{3,4},{4,5},{5,6},{6,7},{7,8},{8,9},{9,10},{10,1... | collective-permute-start | bytes 1572872 | tf_op jit(solution)/shard_map/while/body/eval_jaxpr/ppermute | solution.py:15
  127.8 15.5 collective-permute-start
  127.8 12.4 collective-permute-start.1
  154.3 17.5 collective-permute-start.2
  155.1 12.7 collective-permute-start
  155.1 9.6 collective-permute-start.1
  173.9 32.3 %collective-permute-start.2 = (f32[128,1024]{0,1:T(8,128)}, f32[128,1024]{0,1:T(8,128)}, u32[]{:S(2)}, u32[]{:S(2)}) collective-permute-start(f32[128,1024]{0,1:T(8,128)} %get-tuple-element.464), channel_id=1, source_target_pairs={{0,1},{1,2},{2,3},{3,4},{4,5},{5,6},{6,7},{7,8},{8,9},{9,10},{10,1... | collective-permute-start | bytes 1572872 | tf_op jit(solution)/shard_map/while/body/eval_jaxpr/ppermute | solution.py:15
  177.5 19.7 %collective-permute-start = (bf16[128,1024]{0,1:T(8,128)(2,1)}, bf16[128,1024]{0,1:T(8,128)(2,1)S(1)}, u32[]{:S(2)}, u32[]{:S(2)}) collective-permute-start(bf16[128,1024]{0,1:T(8,128)(2,1)} %get-tuple-element.462), channel_id=1, source_target_pairs={{0,1},{1,2},{2,3},{3,4},{4,5},{5,6},{6,7},{7,8},{8,9},{9,10},{10,1... | collective-permute-start | bytes 786440 | tf_op jit(solution)/shard_map/while/body/eval_jaxpr/ppermute | solution.py:15
  178.9 15.3 collective-permute-start.1
  208.2 17.5 collective-permute-start.2
  208.2 13.4 collective-permute-start
  208.2 10.4 collective-permute-start.1
  227.8 29.0 %collective-permute-start.2 = (f32[128,1024]{0,1:T(8,128)}, f32[128,1024]{0,1:T(8,128)}, u32[]{:S(2)}, u32[]{:S(2)}) collective-permute-start(f32[128,1024]{0,1:T(8,128)} %get-tuple-element.464), channel_id=1, source_target_pairs={{0,1},{1,2},{2,3},{3,4},{4,5},{5,6},{6,7},{7,8},{8,9},{9,10},{10,1... | collective-permute-start | bytes 1572872 | tf_op jit(solution)/shard_map/while/body/eval_jaxpr/ppermute | solution.py:15
  235.5 12.3 collective-permute-start
  235.6 9.2 collective-permute-start.1
  258.9 16.4 collective-permute-start.2
  258.9 12.3 collective-permute-start
  263.4 4.7 collective-permute-start.1
  277.3 31.7 %collective-permute-start.2 = (f32[128,1024]{0,1:T(8,128)}, f32[128,1024]{0,1:T(8,128)}, u32[]{:S(2)}, u32[]{:S(2)}) collective-permute-start(f32[128,1024]{0,1:T(8,128)} %get-tuple-element.464), channel_id=1, source_target_pairs={{0,1},{1,2},{2,3},{3,4},{4,5},{5,6},{6,7},{7,8},{8,9},{9,10},{10,1... | collective-permute-start | bytes 1572872 | tf_op jit(solution)/shard_map/while/body/eval_jaxpr/ppermute | solution.py:15
  281.2 18.8 %collective-permute-start = (bf16[128,1024]{0,1:T(8,128)(2,1)}, bf16[128,1024]{0,1:T(8,128)(2,1)S(1)}, u32[]{:S(2)}, u32[]{:S(2)}) collective-permute-start(bf16[128,1024]{0,1:T(8,128)(2,1)} %get-tuple-element.462), channel_id=1, source_target_pairs={{0,1},{1,2},{2,3},{3,4},{4,5},{5,6},{6,7},{7,8},{8,9},{9,10},{10,1... | collective-permute-start | bytes 786440 | tf_op jit(solution)/shard_map/while/body/eval_jaxpr/ppermute | solution.py:15
  281.9 15.1 collective-permute-start.1
  311.1 27.4 %collective-permute-start.2 = (f32[128,1024]{0,1:T(8,128)}, f32[128,1024]{0,1:T(8,128)}, u32[]{:S(2)}, u32[]{:S(2)}) collective-permute-start(f32[128,1024]{0,1:T(8,128)} %get-tuple-element.464), channel_id=1, source_target_pairs={{0,1},{1,2},{2,3},{3,4},{4,5},{5,6},{6,7},{7,8},{8,9},{9,10},{10,1... | collective-permute-start | bytes 1572872 | tf_op jit(solution)/shard_map/while/body/eval_jaxpr/ppermute | solution.py:15
  311.1 18.4 %collective-permute-start = (bf16[128,1024]{0,1:T(8,128)(2,1)}, bf16[128,1024]{0,1:T(8,128)(2,1)S(1)}, u32[]{:S(2)}, u32[]{:S(2)}) collective-permute-start(bf16[128,1024]{0,1:T(8,128)(2,1)} %get-tuple-element.462), channel_id=1, source_target_pairs={{0,1},{1,2},{2,3},{3,4},{4,5},{5,6},{6,7},{7,8},{8,9},{9,10},{10,1... | collective-permute-start | bytes 786440 | tf_op jit(solution)/shard_map/while/body/eval_jaxpr/ppermute | solution.py:15
  311.1 15.3 collective-permute-start.1
  340.5 27.4 %collective-permute-start.2 = (f32[128,1024]{0,1:T(8,128)}, f32[128,1024]{0,1:T(8,128)}, u32[]{:S(2)}, u32[]{:S(2)}) collective-permute-start(f32[128,1024]{0,1:T(8,128)} %get-tuple-element.464), channel_id=1, source_target_pairs={{0,1},{1,2},{2,3},{3,4},{4,5},{5,6},{6,7},{7,8},{8,9},{9,10},{10,1... | collective-permute-start | bytes 1572872 | tf_op jit(solution)/shard_map/while/body/eval_jaxpr/ppermute | solution.py:15
  340.5 18.4 %collective-permute-start = (bf16[128,1024]{0,1:T(8,128)(2,1)}, bf16[128,1024]{0,1:T(8,128)(2,1)S(1)}, u32[]{:S(2)}, u32[]{:S(2)}) collective-permute-start(bf16[128,1024]{0,1:T(8,128)(2,1)} %get-tuple-element.462), channel_id=1, source_target_pairs={{0,1},{1,2},{2,3},{3,4},{4,5},{5,6},{6,7},{7,8},{8,9},{9,10},{10,1... | collective-permute-start | bytes 786440 | tf_op jit(solution)/shard_map/while/body/eval_jaxpr/ppermute | solution.py:15
  340.5 15.3 collective-permute-start.1
  369.9 27.4 %collective-permute-start.2 = (f32[128,1024]{0,1:T(8,128)}, f32[128,1024]{0,1:T(8,128)}, u32[]{:S(2)}, u32[]{:S(2)}) collective-permute-start(f32[128,1024]{0,1:T(8,128)} %get-tuple-element.464), channel_id=1, source_target_pairs={{0,1},{1,2},{2,3},{3,4},{4,5},{5,6},{6,7},{7,8},{8,9},{9,10},{10,1... | collective-permute-start | bytes 1572872 | tf_op jit(solution)/shard_map/while/body/eval_jaxpr/ppermute | solution.py:15
  369.9 18.4 %collective-permute-start = (bf16[128,1024]{0,1:T(8,128)(2,1)}, bf16[128,1024]{0,1:T(8,128)(2,1)S(1)}, u32[]{:S(2)}, u32[]{:S(2)}) collective-permute-start(bf16[128,1024]{0,1:T(8,128)(2,1)} %get-tuple-element.462), channel_id=1, source_target_pairs={{0,1},{1,2},{2,3},{3,4},{4,5},{5,6},{6,7},{7,8},{8,9},{9,10},{10,1... | collective-permute-start | bytes 786440 | tf_op jit(solution)/shard_map/while/body/eval_jaxpr/ppermute | solution.py:15
  369.9 15.3 collective-permute-start.1
  399.3 27.4 %collective-permute-start.2 = (f32[128,1024]{0,1:T(8,128)}, f32[128,1024]{0,1:T(8,128)}, u32[]{:S(2)}, u32[]{:S(2)}) collective-permute-start(f32[128,1024]{0,1:T(8,128)} %get-tuple-element.464), channel_id=1, source_target_pairs={{0,1},{1,2},{2,3},{3,4},{4,5},{5,6},{6,7},{7,8},{8,9},{9,10},{10,1... | collective-permute-start | bytes 1572872 | tf_op jit(solution)/shard_map/while/body/eval_jaxpr/ppermute | solution.py:15
  399.3 18.4 %collective-permute-start = (bf16[128,1024]{0,1:T(8,128)(2,1)}, bf16[128,1024]{0,1:T(8,128)(2,1)S(1)}, u32[]{:S(2)}, u32[]{:S(2)}) collective-permute-start(bf16[128,1024]{0,1:T(8,128)(2,1)} %get-tuple-element.462), channel_id=1, source_target_pairs={{0,1},{1,2},{2,3},{3,4},{4,5},{5,6},{6,7},{7,8},{8,9},{9,10},{10,1... | collective-permute-start | bytes 786440 | tf_op jit(solution)/shard_map/while/body/eval_jaxpr/ppermute | solution.py:15
  399.3 15.3 collective-permute-start.1
  428.7 11.3 collective-permute-start.3
Sparse Core Ops, SparseCore 0:
  465.7 1305.0 reduce-scatter.3
where the time goes:
time: 1790 us; the launch traced here: 1780 us
  waiting for transfers between devices  1430 us (80%)
  starting transfers between devices  93.3 us (5%)
  other arithmetic  87.7 us (5%)
  loops' own time  59.3 us (3%)
  local copies, waits for them, and re-layouts  52 us (3%)
  matrix products  37.5 us (2%)
    unnamed x2, waiting for transfers between devices  1300 us
    ppermute x46, waiting for transfers between devices, shifted(): return lax.ppermute(value, axis, pairs)  131 us
    ppermute x46, starting transfers between devices, shifted(): return lax.ppermute(value, axis, pairs)  93.3 us
    add x30, other arithmetic, cycle_turn(): return (block_kv, block_tags, kv_acc + kv_part, query_acc + query_part)  66.3 us
    another operation x1, loops' own time, shards(): lax.fori_loop(1, lax.axis_size('cp'), cycle_turn, (key_value, plan_tags,...  37.7 us
  transfers between devices with their start and end apart: 47, of which 17 were waited for; matrix products, arithmetic and copies ran while one was open for 6% of the time, Pallas kernels for 0%

commit v1 on v0

v1 whole, which is shorter than its diff:
```python
import math

import jax
import jax.numpy as jnp
import numpy as np
from jax import lax
from jax.experimental import pallas as pl
from jax.experimental.pallas import tpu as pltpu
from jax.sharding import PartitionSpec as P

MESH = pl.DeviceIdType.MESH
F32 = jnp.float32
BF16 = jnp.bfloat16
ROPE_BASE = 500000.0
DH = 128
T = 128
N_CP = 16
N_DP = 16
SCALE = 1.0 / math.sqrt(DH)
LOG2E = math.log2(math.e)


def rope_tables():
    half = DH // 2
    freq = (ROPE_BASE ** (-(np.arange(half) * 2.0 / DH))).astype(np.float32)
    angles = (np.arange(N_CP * T, dtype=np.float32)[:, None] * freq[None, :]).astype(np.float32)
    cosine = np.cos(angles.astype(np.float64))
    sine = np.sin(angles.astype(np.float64))
    cos_table = np.concatenate([cosine, cosine], axis=1).astype(np.float32)
    sin_table = np.concatenate([sine, -sine], axis=1).astype(np.float32)
    return cos_table.reshape(N_CP, T, DH), sin_table.reshape(N_CP, T, DH)


def dot(a, b, ca, cb):
    return lax.dot_general(a, b, (((ca,), (cb,)), ((), ())), preferred_element_type=F32)


def kernel(
    x_hbm, q_hbm, k_hbm, v_hbm, o_hbm, g_hbm, lse_ref, first_ref, span_ref, length_ref, cos_hbm, sin_hbm,
    dq_out, w_out,
    x_v, o_v, g_v, cos_v, sin_v,
    qbuf, gbuf, kbuf, vbuf, stbuf, tagbuf, st_src, tag_src, tags_s, sig_s,
    qs, gs, ks, vs, kts, st_s, dqt, dkv_s,
    xts, xbuf, core_src, core_buf, rs_src, rs_buf, kvbuf,
    dq_s, dq_src, w_src, w_core, wsend, wbuf,
    lsem, asem_s, asem_r, xsem_s, xsem_r, ksem_s, ksem_r, wsem_s, wsem_r, dsem_s, dsem_r,
):
    r = lax.axis_index("dp")
    c = lax.axis_index("cp")
    x, y, q = c // 4, (c // 2) % 2, c % 2
    head = 8 * y + 2 * x + q
    mate = x * 4 + y * 2 + (1 - q)

    barrier = pltpu.get_barrier_semaphore()

    def greet_row(d, _):
        pl.semaphore_signal(barrier, inc=1, device_id=(r, (c + d) % N_CP), device_id_type=MESH)
        return 0

    lax.fori_loop(1, N_CP, greet_row, 0)

    def greet_far(i, _):
        rd = (r + 1 + i // 2) % N_DP
        cd = x * 4 + (i % 2) * 2 + q
        pl.semaphore_signal(barrier, inc=1, device_id=(rd, cd), device_id_type=MESH)
        return 0

    lax.fori_loop(0, 2 * (N_DP - 1), greet_far, 0)

    own = pl.ds(head * DH, DH)
    own_kv = pl.ds((head // 4) * DH, DH)
    loads = [
        pltpu.make_async_copy(o_hbm, o_v, lsem.at[0]),
        pltpu.make_async_copy(g_hbm, g_v, lsem.at[1]),
        pltpu.make_async_copy(x_hbm, x_v, lsem.at[2]),
        pltpu.make_async_copy(cos_hbm, cos_v, lsem.at[3]),
        pltpu.make_async_copy(sin_hbm, sin_v, lsem.at[4]),
        pltpu.make_async_copy(q_hbm.at[:, own], qbuf.at[c], lsem.at[5]),
        pltpu.make_async_copy(g_hbm.at[:, own], gbuf.at[c], lsem.at[6]),
        pltpu.make_async_copy(k_hbm.at[:, own_kv], kbuf.at[c], lsem.at[7]),
        pltpu.make_async_copy(v_hbm.at[:, own_kv], vbuf.at[c], lsem.at[8]),
    ]
    for load in loads:
        load.start()

    pl.semaphore_wait(barrier, (N_CP - 1) + 2 * (N_DP - 1))

    def row_peer(d):
        xd, yd, qd = (x + d // 4) % 4, (y + (d // 2) % 2) % 2, (q + d % 2) % 2
        return xd, yd, qd, xd * 4 + yd * 2 + qd

    def remote(src, dst, send, recv, rd, cd):
        return pltpu.make_async_remote_copy(
            src_ref=src, dst_ref=dst, send_sem=send, recv_sem=recv, device_id=(rd, cd), device_id_type=MESH
        )

    def take(ref, sem):
        pltpu.make_async_copy(ref, ref, sem).wait()

    def send_heads(d, _):
        xd, yd, qd, cd = row_peer(d)
        hd = 8 * yd + 2 * xd + qd
        cols = pl.ds(hd * DH, DH)
        kv_cols = pl.ds((hd // 4) * DH, DH)
        remote(q_hbm.at[:, cols], qbuf.at[c], asem_s.at[0], asem_r.at[0], r, cd).start()
        remote(k_hbm.at[:, kv_cols], kbuf.at[c], asem_s.at[1], asem_r.at[1], r, cd).start()
        remote(g_hbm.at[:, cols], gbuf.at[c], asem_s.at[2], asem_r.at[2], r, cd).start()
        remote(v_hbm.at[:, kv_cols], vbuf.at[c], asem_s.at[3], asem_r.at[3], r, cd).start()
        return 0

    lax.fori_loop(1, N_CP, send_heads, 0)

    first = first_ref[0, 0]
    span = span_ref[0, 0]
    length = length_ref[0, 0]
    row_id = lax.broadcasted_iota(jnp.int32, (8, T), 0)
    tag_src[...] = jnp.where(row_id == 0, first + span, jnp.where(row_id == 1, first, 0))
    pos = span * T + lax.broadcasted_iota(jnp.int32, (1, T), 1)
    low = jnp.where(pos < length, first * T, 2 * N_CP * T).astype(F32)
    lse_t = jnp.concatenate([lse_ref[...] * LOG2E, jnp.zeros((T, T - 16), F32)], axis=1).T
    for load in loads[:2]:
        load.wait()
    lane = lax.broadcasted_iota(jnp.int32, (T, T), 1)
    delta = jnp.zeros((T, T), F32)
    for h in range(16):
        cols = slice(h * DH, (h + 1) * DH)
        part = jnp.sum(o_v[:, cols].astype(F32) * g_v[:, cols].astype(F32), axis=1, keepdims=True)
        delta = jnp.where(lane == h, part, delta)
    delta_t = delta.T
    for h in range(16):
        rows = jnp.concatenate([lse_t[h : h + 1], delta_t[h : h + 1], low, jnp.zeros((5, T), F32)], axis=0)
        st_src[h] = rows

    def send_stats(d, _):
        xd, yd, qd, cd = row_peer(d)
        hd = 8 * yd + 2 * xd + qd
        remote(st_src.at[hd], stbuf.at[c], asem_s.at[4], asem_r.at[4], r, cd).start()
        remote(tag_src, tagbuf.at[c], asem_s.at[5], asem_r.at[5], r, cd).start()
        return 0

    lax.fori_loop(1, N_CP, send_stats, 0)
    stbuf[c] = st_src[head]
    tagbuf[c] = tag_src[...]

    loads[2].wait()

    def turn_x(b, _):
        for part in range(2):
            block = x_v[:, pl.ds(pl.multiple_of(b * 256 + part * 128, 128), 128)].T
            for k in range(8):
                owner = part * 8 + k
                start = (owner % 2) * 512 + ((owner // 2) % 2) * 256 + b * 16
                xts[owner // 4, pl.ds(pl.multiple_of(start, 16), 16), :] = block[k * 16 : (k + 1) * 16]
        return 0

    lax.fori_loop(0, N_DP, turn_x, 0)

    for load in loads[3:]:
        load.wait()
    for i, buf in enumerate((qbuf, kbuf, gbuf, vbuf, stbuf, tagbuf)):
        take(buf.at[pl.ds(0, N_CP - 1)], asem_r.at[i])

    slot_u, slot_m = x // 2, (x % 2) * 2 + y

    def send_x(d, _):
        xd, yd = (x + d // 2) % 4, (y + d % 2) % 2
        dst = xbuf.at[slot_u, :, pl.ds(pl.multiple_of(slot_m * T, T), T)]
        remote(xts.at[xd], dst, xsem_s, xsem_r, r, xd * 4 + yd * 2 + q).start()
        return 0

    lax.fori_loop(1, 8, send_x, 0)
    keep = pltpu.make_async_copy(
        xts.at[x], xbuf.at[slot_u, :, pl.ds(pl.multiple_of(slot_m * T, T), T)], lsem.at[0]
    )
    keep.start()

    tag_load = pltpu.make_async_copy(tagbuf, tags_s, lsem.at[1])
    tag_load.start()
    tag_load.wait()
    place = [tags_s[m, 0, 0] for m in range(N_CP)]
    for p in range(N_CP):
        m = jnp.int32(0)
        for i in range(1, N_CP):
            m = jnp.where(place[i] == p, i, m)
        sig_s[p] = p - tags_s[m, 1, 0]
        qs[p] = qbuf[m]
        gs[p] = gbuf[m]
        vs[p] = vbuf[m]
        key = kbuf[m]
        ks[p] = key
        kts[p // 2, :, (p % 2) * T : (p % 2 + 1) * T] = key.T
        st_s[p // 2, :, (p % 2) * T : (p % 2 + 1) * T] = stbuf[m]
    dqt[...] = jnp.zeros_like(dqt)

    def key_block(step, _):
        kb = 7 - step
        key = ks[pl.ds(2 * kb, 2)].reshape(256, DH)
        value = vs[pl.ds(2 * kb, 2)].reshape(256, DH)
        key_t = kts[kb]

        def unit(qb, carry, diagonal):
            dk, dv = carry
            query = qs[pl.ds(2 * qb, 2)].reshape(256, DH)
            grad = gs[pl.ds(2 * qb, 2)].reshape(256, DH)
            stats = st_s[qb]
            scores = dot(key, query, 1, 1)
            dp = dot(value, grad, 1, 1)
            s_at = lax.broadcasted_iota(jnp.int32, (256, 256), 0)
            allowed = s_at >= stats[2:3].astype(jnp.int32) - kb * 256
            if diagonal:
                allowed = allowed & (s_at <= lax.broadcasted_iota(jnp.int32, (256, 256), 1))
            probs = jnp.where(allowed, jnp.exp2(scores * (SCALE * LOG2E) - stats[0:1]), 0.0)
            ds = (probs * (dp - stats[1:2])).astype(BF16)
            dv = dv + dot(probs.astype(BF16), grad, 1, 0)
            dk = dk + dot(ds, query, 1, 0)
            dqt[qb] += dot(key_t, ds, 1, 0)
            return dk, dv

        zero = jnp.zeros((256, DH), F32)
        carry = unit(kb, (zero, zero), True)
        dk, dv = lax.fori_loop(kb + 1, 8, lambda qb, cc: unit(qb, cc, False), carry)
        for i in range(2):
            p = 2 * kb + i
            rows = slice(i * T, (i + 1) * T)
            turned = dk[rows] * SCALE
            sig = sig_s[p]
            plain = turned * cos_v[sig] + pltpu.roll(turned, DH // 2, 1) * sin_v[sig]
            dkv_s[p] = jnp.concatenate([plain, dv[rows]], axis=1).astype(BF16)
        return 0

    lax.fori_loop(0, 8, key_block, 0)

    for e in range(8):
        core_src[e] = dkv_s[tags_s[2 * e + (1 - q), 0, 0]]
    to_mate = remote(core_src, core_buf, ksem_s.at[0], ksem_r.at[0], r, mate)
    to_mate.start()

    for p in range(N_CP):
        dq_s[p] = (dqt[p // 2, :, (p % 2) * T : (p % 2 + 1) * T] * SCALE).T.astype(BF16)
    for m in range(N_CP):
        dq_src[m] = dq_s[place[m]]

    to_mate.wait()
    g, u = x // 2, x % 2
    for e in range(4):
        give = 4 * (1 - u) + e
        summed = dkv_s[tags_s[2 * give + q, 0, 0]].astype(F32) + core_buf[give].astype(F32)
        rs_src[e] = summed.astype(BF16)
    pair = (x // 2) * 2 + (1 - u)
    to_pair = remote(rs_src, rs_buf, ksem_s.at[1], ksem_r.at[1], r, pair * 4 + y * 2 + q)
    to_pair.start()
    to_pair.wait()
    for e in range(4):
        mine = 4 * u + e
        summed = dkv_s[tags_s[2 * mine + q, 0, 0]].astype(F32) + core_buf[mine].astype(F32)
        kvbuf[x, pl.ds(e * T, T), :] = (summed + rs_buf[e].astype(F32)).astype(BF16)
    shares = []
    for d in range(1, 4):
        cd = ((x + d) % 4) * 4 + y * 2 + q
        share = remote(kvbuf.at[x], kvbuf.at[x], ksem_s.at[1 + d], ksem_r.at[1 + d], r, cd)
        share.start()
        shares.append(share)

    def send_dq(d, _):
        xd, yd, qd, cd = row_peer(d)
        remote(dq_src.at[cd], dq_out.at[:, own], dsem_s, dsem_r, r, cd).start()
        return 0

    lax.fori_loop(1, N_CP, send_dq, 0)
    dq_keep = pltpu.make_async_copy(dq_src.at[c], dq_out.at[:, own], lsem.at[2])
    dq_keep.start()

    take(xbuf.at[:, pl.ds(0, 7 * T), :], xsem_r)
    keep.wait()
    for share in shares:
        share.wait()

    def tile(start, gg):
        rows = pl.ds(pl.multiple_of(start, 256), 256)
        return dot(xbuf[0, rows, :], kvbuf[2 * gg], 1, 0) + dot(xbuf[1, rows, :], kvbuf[2 * gg + 1], 1, 0)

    for yo in range(2):
        for gg in range(2):
            w_src[yo * 256 : (yo + 1) * 256, gg * 256 : (gg + 1) * 256] = tile(
                (1 - q) * 512 + yo * 256, gg
            ).astype(BF16)
    w_mate = remote(w_src, w_core, wsem_s.at[0], wsem_r.at[0], r, mate)
    w_mate.start()
    w_mate.wait()
    for yo in range(2):
        for gg in range(2):
            block = tile(q * 512 + yo * 256, gg) + w_core[
                yo * 256 : (yo + 1) * 256, gg * 256 : (gg + 1) * 256
            ].astype(F32)
            wsend[yo, :, :, gg * 256 : (gg + 1) * 256] = block.astype(BF16).reshape(N_DP, 16, 256)

    def send_w(i, _):
        rd, yd = (r + i // 2) % N_DP, (y + i % 2) % 2
        remote(wsend.at[yd, rd], wbuf.at[2 * r + y], wsem_s.at[1], wsem_r.at[1], rd, x * 4 + yd * 2 + q).start()
        return 0

    lax.fori_loop(1, 2 * N_DP, send_w, 0)
    wbuf[2 * r + y] = wsend[y, r]
    take(wbuf.at[pl.ds(0, 2 * N_DP - 1)], wsem_r.at[1])
    for yy in range(2):
        total = lax.fori_loop(
            1, N_DP, lambda i, t: t + wbuf[2 * i + yy].astype(F32), wbuf[yy].astype(F32)
        )
        for gg in range(2):
            j = 2 * yy + gg
            w_out[:, j * DH : (j + 1) * DH] = total[:, gg * 256 : gg * 256 + DH].astype(BF16)
            w_out[:, 512 + j * DH : 512 + (j + 1) * DH] = total[:, gg * 256 + DH : (gg + 1) * 256].astype(BF16)

    take(dq_src.at[pl.ds(0, N_CP - 1)], dsem_r)
    take(dq_src.at[pl.ds(0, N_CP - 1)], dsem_s)
    dq_keep.wait()
    for i, buf in enumerate((qbuf, kbuf, gbuf, vbuf, stbuf, tagbuf)):
        take(buf.at[pl.ds(0, N_CP - 1)], asem_s.at[i])
    take(xbuf.at[:, pl.ds(0, 7 * T), :], xsem_s)
    take(wbuf.at[pl.ds(0, 2 * N_DP - 1)], wsem_s.at[1])


def shards(layer_input, queries, keys, values, outputs, out_grad, log_sum_exp, group_first, span_index, seq_length):
    cos_table, sin_table = rope_tables()
    anywhere = pl.BlockSpec(memory_space=pl.ANY)
    vmem = pl.BlockSpec(memory_space=pltpu.VMEM)
    smem = pl.BlockSpec(memory_space=pltpu.SMEM)
    dma = pltpu.SemaphoreType.DMA
    V = pltpu.VMEM
    scratch = [
        V((T, 4096), BF16), V((T, 2048), BF16), V((T, 2048), BF16), V((16, T, DH), F32), V((16, T, DH), F32),
        V((16, T, DH), BF16), V((16, T, DH), BF16), V((16, T, DH), BF16), V((16, T, DH), BF16),
        V((16, 8, T), F32), V((16, 8, T), jnp.int32), V((16, 8, T), F32), V((8, T), jnp.int32),
        pltpu.SMEM((16, 8, T), jnp.int32), pltpu.SMEM((16,), jnp.int32),
        V((16, T, DH), BF16), V((16, T, DH), BF16), V((16, T, DH), BF16), V((16, T, DH), BF16),
        V((8, DH, 256), BF16), V((8, 8, 256), F32), V((8, DH, 256), F32), V((16, T, 256), BF16),
        V((4, 1024, T), BF16), V((2, 1024, 512), BF16), V((8, T, 256), BF16), V((8, T, 256), BF16),
        V((4, T, 256), BF16), V((4, T, 256), BF16), V((4, 512, 256), BF16),
        V((16, T, DH), BF16), V((16, T, DH), BF16), V((512, 512), BF16), V((512, 512), BF16),
        V((2, 16, 16, 512), BF16), V((32, 16, 512), BF16),
        dma((9,)), dma((6,)), dma((6,)), dma, dma, dma((5,)), dma((5,)), dma((2,)), dma((2,)), dma, dma,
    ]
    return pl.pallas_call(
        kernel,
        out_shape=(
            jax.ShapeDtypeStruct((T, 2048), BF16),
            jax.ShapeDtypeStruct((16, 1024), BF16),
        ),
        in_specs=[anywhere] * 6 + [vmem, smem, smem, smem, anywhere, anywhere],
        out_specs=(anywhere, vmem),
        scratch_shapes=scratch,
        compiler_params=pltpu.CompilerParams(
            collective_id=0, has_side_effects=True, vmem_limit_bytes=48 * 1024 * 1024
        ),
        name="attention_backward",
    )(
        layer_input, queries, keys, values, outputs, out_grad, log_sum_exp,
        group_first, span_index, seq_length, jnp.asarray(cos_table), jnp.asarray(sin_table),
    )


def solution(mesh):
    both = P(("dp", "cp"), None)
    placed = (both,) * 7 + (P("dp", "cp"),) * 3
    return jax.shard_map(shards, mesh=mesh, in_specs=placed, out_specs=(both, both), check_vma=False)
```

time: 1790 us -> 126 us (0.07)
  waiting for transfers between devices: 1430 us -> 0 us
  Pallas kernels: 0 us -> 112 us
  starting transfers between devices: 93.3 us -> 0 us
  other arithmetic: 87.7 us -> 0 us
  loops' own time: 59.3 us -> 0 us
  local copies, waits for them, and re-layouts: 52 us -> 10.8 us
  matrix products: 37.5 us -> 0 us
    unnamed x2 -> x0, waiting for transfers between devices: 1300 us -> none
    ppermute x46 -> x0, waiting for transfers between devices: 131 us -> none  [shifted(): return lax.ppermute(value, axis, pairs)]
    pallas_call x0 -> x1, Pallas kernels: none -> 112 us  [shards(): pl.pallas_call(kernel, out_shape=(jax.ShapeDtypeStruct((T, 2048), BF16),...]
    ppermute x46 -> x0, starting transfers between devices: 93.3 us -> none  [shifted(): return lax.ppermute(value, axis, pairs)]
    add x43 -> x0, other arithmetic: 66.3 us -> none  [the longest x30 66.3 us: cycle_turn(): return (block_kv, block_tags, kv_acc + kv_part, query_acc + query_part)]
    another operation x17 -> x0, loops' own time: 59.3 us -> none  [the longest x1 37.7 us: shards(): lax.fori_loop(1, lax.axis_size('cp'), cycle_turn, (key_value, plan_tags,...]
    dot_general x61 -> x0, matrix products: 37.5 us -> none  [the longest x12 13.1 us: grad_tables(): jnp.einsum('qhgd,khd->hgqk', query_heads, key_block, preferred_element_ty...]
  transfers between devices with their start and end apart: 47 -> 0, of which waited for: 17 -> 0; matrix products, arithmetic and copies ran while one was open for 6% -> 0% of each run, Pallas kernels for 0% -> 0%
where the time goes in v1:
time: 126 us
  Pallas kernels  112 us (89%)
  local copies, waits for them, and re-layouts  10.8 us (9%)
  between operations  2.59 us (2%)
    pallas_call x1, Pallas kernels, shards(): pl.pallas_call(kernel, out_shape=(jax.ShapeDtypeStruct((T, 2048), BF16),...  112 us
    unnamed x19, local copies, waits for them, and re-layouts  10.8 us

profile of v1, /device:TPU:1, one launch (start us, length us, event | category | flops | bytes accessed | tf_op | source)
XLA Modules:
  0.0 125.9 jit_solution(9624073549870171960)
XLA Ops:
  2.6 0.8 copy.14.lse_ref
  3.4 0.0 copy-start
  3.4 1.2 copy-done
  4.6 0.0 copy-start.1
  4.6 1.2 copy-done.1
  5.8 0.0 copy-start.2
  5.8 1.2 copy-done.2
  7.0 0.0 copy-start.3
  7.0 1.0 copy-done.3
  8.1 0.0 copy-start.4
  8.1 1.0 copy-done.4
  9.1 0.0 copy-start.5
  9.1 1.0 copy-done.5
  10.2 0.0 copy-start.6
  10.2 0.9 copy-done.6
  11.1 0.0 copy-start.7
  11.1 0.9 copy-done.7
  12.0 112.5 %attention_backward.1 = (bf16[128,2048]{1,0:T(8,128)(2,1)S(1)}, bf16[16,1024]{1,0:T(8,128)(2,1)S(1)}) custom-call(bf16[128,4096]{1,0:T(8,128)(2,1)S(1)} %copy-done, bf16[128,2048]{1,0:T(8,128)(2,1)S(1)} %copy-done.3, bf16[128,512]{1,0:T(8,128)(2,1)S(1)} %copy-done.6, bf16[128,512]{1,0:T(8,128)(2,1)S(1)} %copy-done.7, bf16[128,2048]{1,0:T(8,128)(2,1)S(1)} %copy-done.4, ...), custom_call_target="tpu_custom_call" | custom-call | tf_op jit(solution)/shard_map/attention_backward/pallas_call | solution.py:343
  124.5 0.8 copy.20
  125.3 0.6 copy.21
Async XLA Ops:
  3.4 1.2 copy-start
  4.6 1.2 copy-start.1
  5.8 1.2 copy-start.2
  7.0 1.0 copy-start.3
  8.1 1.0 copy-start.4
  9.1 1.0 copy-start.5
  10.2 0.9 copy-start.6
  11.1 0.9 copy-start.7

commit v2 on v1

v2 whole, which is shorter than its diff:
```python
import math

import jax
import jax.numpy as jnp
import numpy as np
from jax import lax
from jax.experimental import pallas as pl
from jax.experimental.pallas import tpu as pltpu
from jax.sharding import PartitionSpec as P

MESH = pl.DeviceIdType.MESH
F32 = jnp.float32
BF16 = jnp.bfloat16
ROPE_BASE = 500000.0
DH = 128
T = 128
N_CP = 16
N_DP = 16
SCALE = 1.0 / math.sqrt(DH)
LOG2E = math.log2(math.e)
NT = 4
BL = NT * T
NB = N_CP // NT
ORDER = (6, 14, 10, 2, 4, 12, 8, 3, 7, 15, 11, 5, 13, 9, 1)
FAR = (4, 3, 5, 2, 6, 1, 7)


def rope_tables():
    half = DH // 2
    freq = (ROPE_BASE ** (-(np.arange(half) * 2.0 / DH))).astype(np.float32)
    angles = (np.arange(N_CP * T, dtype=np.float32)[:, None] * freq[None, :]).astype(np.float32)
    cosine = np.cos(angles.astype(np.float64))
    sine = np.sin(angles.astype(np.float64))
    cos_table = np.concatenate([cosine, cosine], axis=1).astype(np.float32)
    sin_table = np.concatenate([sine, -sine], axis=1).astype(np.float32)
    return cos_table.reshape(N_CP, T, DH), sin_table.reshape(N_CP, T, DH)


def dot(a, b, ca, cb):
    return lax.dot_general(a, b, (((ca,), (cb,)), ((), ())), preferred_element_type=F32)


def kernel(
    x_hbm, q_hbm, k_hbm, v_hbm, o_hbm, g_hbm, lse_ref, first_ref, span_ref, length_ref, cos_hbm, sin_hbm,
    dq_out, w_out,
    x_v, o_v, g_v, cos_v, sin_v,
    qbuf, gbuf, kvbuf_in, stbuf, tagbuf, st_src, tag_src, tags_s, sig_s,
    qs, gs, kvs, kts, st_s, dqt, dkv_s,
    xts, xbuf, core_src, core_buf, rs_src, rs_buf, kvbuf,
    dq_s, dq_src, w_src, w_core, w_own, wsend, wbuf, wsum, wpart,
    lsem, asem_s, asem_r, xsem_s, xsem_r, ksem_s, ksem_r, wsem_s, wsem_r, dsem_s, dsem_r,
):
    r = lax.axis_index("dp")
    c = lax.axis_index("cp")
    x, y, q = c // 4, (c // 2) % 2, c % 2
    head = 8 * y + 2 * x + q
    mate = x * 4 + y * 2 + (1 - q)

    barrier = pltpu.get_barrier_semaphore()
    z, low_y = r // 2, r % 2
    beside = z * 2 + 1 - low_y
    y_mate = x * 4 + (1 - y) * 2 + q

    def greet(rd, cd):
        pl.semaphore_signal(barrier, inc=1, device_id=(rd, cd), device_id_type=MESH)

    for d in range(1, N_CP):
        greet(r, (c + d) % N_CP)
    for dz in FAR:
        greet(((z + dz) % 8) * 2 + low_y, c)
    greet(beside, c)
    greet(beside, y_mate)

    own = pl.ds(head * DH, DH)
    own_kv = pl.ds((head // 4) * DH, DH)
    kv_hbm = (k_hbm, v_hbm)
    loads = [
        pltpu.make_async_copy(o_hbm, o_v, lsem.at[0]),
        pltpu.make_async_copy(g_hbm, g_v, lsem.at[1]),
        pltpu.make_async_copy(x_hbm, x_v, lsem.at[2]),
        pltpu.make_async_copy(cos_hbm, cos_v, lsem.at[3]),
        pltpu.make_async_copy(sin_hbm, sin_v, lsem.at[4]),
        pltpu.make_async_copy(q_hbm.at[:, own], qbuf.at[c], lsem.at[5]),
        pltpu.make_async_copy(g_hbm.at[:, own], gbuf.at[c], lsem.at[6]),
    ]
    for load in loads:
        load.start()
    for core in range(2):

        @pl.when(q == core)
        def _():
            pltpu.make_async_copy(kv_hbm[core].at[:, own_kv], kvbuf_in.at[c], lsem.at[7]).start()

    pl.semaphore_wait(barrier, (N_CP - 1) + len(FAR) + 2)

    def row_peer(d):
        xd, yd, qd = (x + d // 4) % 4, (y + (d // 2) % 2) % 2, (q + d % 2) % 2
        return xd, yd, qd, xd * 4 + yd * 2 + qd

    def remote(src, dst, send, recv, rd, cd):
        return pltpu.make_async_remote_copy(
            src_ref=src, dst_ref=dst, send_sem=send, recv_sem=recv, device_id=(rd, cd), device_id_type=MESH
        )

    def take(ref, sem):
        pltpu.make_async_copy(ref, ref, sem).wait()

    first = first_ref[0, 0]
    span = span_ref[0, 0]
    length = length_ref[0, 0]
    row_id = lax.broadcasted_iota(jnp.int32, (8, T), 0)
    tag_src[...] = jnp.where(row_id == 0, first + span, jnp.where(row_id == 1, first, 0))
    for d in ORDER:
        xd, yd, qd, cd = row_peer(d)
        kv_cols = pl.ds((2 * yd + xd // 2) * DH, DH)
        for core in range(2):

            @pl.when(qd == core)
            def _():
                remote(kv_hbm[core].at[:, kv_cols], kvbuf_in.at[c], asem_s.at[1], asem_r.at[1], r, cd).start()

        remote(tag_src, tagbuf.at[c], asem_s.at[4], asem_r.at[4], r, cd).start()

    def send_heads(ref, buf, i):
        for d in ORDER:
            xd, yd, qd, cd = row_peer(d)
            cols = pl.ds((8 * yd + 2 * xd + qd) * DH, DH)
            remote(ref.at[:, cols], buf.at[c], asem_s.at[i], asem_r.at[i], r, cd).start()

    send_heads(q_hbm, qbuf, 0)

    pos = span * T + lax.broadcasted_iota(jnp.int32, (1, T), 1)
    low = jnp.where(pos < length, first * T, 2 * N_CP * T).astype(F32)
    lse_t = jnp.concatenate([lse_ref[...] * LOG2E, jnp.zeros((T, T - 16), F32)], axis=1).T
    for load in loads[:2]:
        load.wait()
    lane = lax.broadcasted_iota(jnp.int32, (T, T), 1)
    delta = jnp.zeros((T, T), F32)
    for h in range(16):
        cols = slice(h * DH, (h + 1) * DH)
        part = jnp.sum(o_v[:, cols].astype(F32) * g_v[:, cols].astype(F32), axis=1, keepdims=True)
        delta = jnp.where(lane == h, part, delta)
    delta_t = delta.T
    for h in range(16):
        rows = jnp.concatenate([lse_t[h : h + 1], delta_t[h : h + 1], low, jnp.zeros((5, T), F32)], axis=0)
        st_src[h] = rows

    def send_stats(d, _):
        xd, yd, qd, cd = row_peer(d)
        hd = 8 * yd + 2 * xd + qd
        remote(st_src.at[hd], stbuf.at[c], asem_s.at[3], asem_r.at[3], r, cd).start()
        return 0

    lax.fori_loop(1, N_CP, send_stats, 0)
    send_heads(g_hbm, gbuf, 2)
    stbuf[c] = st_src[head]
    tagbuf[c] = tag_src[...]

    loads[2].wait()

    def turn_x(b, _):
        for part in range(2):
            block = x_v[:, pl.ds(pl.multiple_of(b * 256 + part * 128, 128), 128)].T
            for k in range(8):
                owner = part * 8 + k
                start = (owner % 2) * 512 + ((owner // 2) % 2) * 256 + b * 16
                xts[owner // 4, pl.ds(pl.multiple_of(start, 16), 16), :] = block[k * 16 : (k + 1) * 16]
        return 0

    lax.fori_loop(0, N_DP, turn_x, 0)

    take(tagbuf.at[pl.ds(0, N_CP - 1)], asem_r.at[4])
    tag_load = pltpu.make_async_copy(tagbuf, tags_s, lsem.at[8])
    tag_load.start()
    tag_load.wait()
    place = [tags_s[m, 0, 0] for m in range(N_CP)]
    member = []
    for p in range(N_CP):
        m = jnp.int32(0)
        for i in range(1, N_CP):
            m = jnp.where(place[i] == p, i, m)
        member.append(m)
        sig_s[p] = p - tags_s[m, 1, 0]

    pltpu.make_async_copy(kvbuf_in.at[c], kvbuf_in.at[c], lsem.at[7]).wait()
    take(kvbuf_in.at[pl.ds(0, N_CP - 1)], asem_r.at[1])
    for p in range(N_CP):
        kvs[q, p] = kvbuf_in[member[p]]
    forward = remote(kvs.at[q], kvs.at[q], lsem.at[9], lsem.at[10], r, mate)
    forward.start()

    for load in loads[3:]:
        load.wait()
    for i, buf in ((0, qbuf), (2, gbuf), (3, stbuf)):
        take(buf.at[pl.ds(0, N_CP - 1)], asem_r.at[i])

    def x_slot(xs, ys):
        lanes = pl.ds(pl.multiple_of(((xs % 2) * 2 + ys) * T, T), T)
        return xbuf.at[xs // 2, :, lanes]

    x_sends = []
    for i, d in enumerate((1, 3, 2)):
        send = remote(xts.at[(x + d) % 4], x_slot(x, y), xsem_s.at[i], xsem_r.at[i], r, ((x + d) % 4) * 4 + y * 2 + q)
        send.start()
        x_sends.append(send)
    keep = pltpu.make_async_copy(xts.at[x], x_slot(x, y), lsem.at[0])
    keep.start()
    across = [remote(xts.at[x], x_slot(x, y), xsem_s.at[3], xsem_r.at[3], r, y_mate)]
    across[0].start()

    def hand_on(i):
        slot = x_slot((x - (1, 3, 2)[i]) % 4, y)
        x_sends[i].wait_recv()
        across.append(remote(slot, slot, xsem_s.at[4 + i], xsem_r.at[4 + i], r, y_mate))
        across[-1].start()

    for p in range(N_CP):
        qs[p] = qbuf[member[p]]
        gs[p] = gbuf[member[p]]
        st_s[p // NT, :, (p % NT) * T : (p % NT + 1) * T] = stbuf[member[p]]
    forward.wait()
    for p in range(N_CP):
        kts[p // NT, :, (p % NT) * T : (p % NT + 1) * T] = kvs[0, p].T
    dqt[...] = jnp.zeros_like(dqt)

    def key_block(step, _):
        kb = NB - 1 - step
        key = kvs[0, pl.ds(NT * kb, NT)].reshape(BL, DH)
        value = kvs[1, pl.ds(NT * kb, NT)].reshape(BL, DH)
        key_t = kts[kb]

        def unit(qb, carry, diagonal):
            dk, dv = carry
            query = qs[pl.ds(NT * qb, NT)].reshape(BL, DH)
            grad = gs[pl.ds(NT * qb, NT)].reshape(BL, DH)
            stats = st_s[qb]
            scores = dot(key, query, 1, 1)
            dp = dot(value, grad, 1, 1)
            s_at = lax.broadcasted_iota(jnp.int32, (BL, BL), 0)
            allowed = s_at >= stats[2:3].astype(jnp.int32) - kb * BL
            if diagonal:
                allowed = allowed & (s_at <= lax.broadcasted_iota(jnp.int32, (BL, BL), 1))
            probs = jnp.where(allowed, jnp.exp2(scores * (SCALE * LOG2E) - stats[0:1]), 0.0)
            ds = (probs * (dp - stats[1:2])).astype(BF16)
            dv = dv + dot(probs.astype(BF16), grad, 1, 0)
            dk = dk + dot(ds, query, 1, 0)
            dqt[qb] += dot(key_t, ds, 1, 0)
            return dk, dv

        zero = jnp.zeros((BL, DH), F32)
        carry = unit(kb, (zero, zero), True)
        dk, dv = lax.fori_loop(kb + 1, NB, lambda qb, cc: unit(qb, cc, False), carry)
        for i in range(NT):
            p = NT * kb + i
            rows = slice(i * T, (i + 1) * T)
            turned = dk[rows] * SCALE
            sig = sig_s[p]
            plain = turned * cos_v[sig] + pltpu.roll(turned, DH // 2, 1) * sin_v[sig]
            dkv_s[p] = jnp.concatenate([plain, dv[rows]], axis=1).astype(BF16)
        return 0

    lax.fori_loop(0, NB - 1, key_block, 0)
    hand_on(0)
    hand_on(1)
    lax.fori_loop(NB - 1, NB, key_block, 0)

    u = x % 2
    pair, other = x + 1 - 2 * u, 3 - x
    pair_dev, other_dev = pair * 4 + y * 2 + q, other * 4 + y * 2 + q

    def k_copy(src, dst, i, k, dev):
        return remote(src, dst, ksem_s.at[i, k], ksem_r.at[i, k], r, dev)

    to_mate = []
    for i, half in enumerate((1 - u, u)):
        for k in range(4):
            e = 4 * half + k
            core_src[i, k] = dkv_s[tags_s[2 * e + (1 - q), 0, 0]]
            to_mate.append(k_copy(core_src.at[i, k], core_buf.at[i, k], i, k, mate))
            to_mate[-1].start()

    def chip_sum(i, k):
        e = 4 * (1 - u if i == 0 else u) + k
        return dkv_s[tags_s[2 * e + q, 0, 0]].astype(F32) + core_buf[i, k].astype(F32)

    to_pair = []
    for k in range(4):
        to_mate[k].wait_recv()
        rs_src[k] = chip_sum(0, k).astype(BF16)
        to_pair.append(k_copy(rs_src.at[k], rs_buf.at[k], 2, k, pair_dev))
        to_pair[-1].start()
    hand_on(2)

    shares, relays = [], []

    def relay(k):
        shares[2 * k].wait_recv()
        relays.append(k_copy(kvbuf.at[pair, k], kvbuf.at[pair, k], 5, k, other_dev))
        relays[-1].start()

    for k in range(4):
        to_mate[4 + k].wait_recv()
        mine = chip_sum(1, k)
        to_pair[k].wait_recv()
        kvbuf[x, k] = (mine + rs_buf[k].astype(F32)).astype(BF16)
        for i, dev in ((3, pair_dev), (4, other_dev)):
            shares.append(k_copy(kvbuf.at[x, k], kvbuf.at[x, k], i, k, dev))
            shares[-1].start()
        if k:
            relay(k - 1)
    relay(3)

    for p in range(N_CP):
        dq_s[p] = (dqt[p // NT, :, (p % NT) * T : (p % NT + 1) * T] * SCALE).T.astype(BF16)
    for m in range(N_CP):
        dq_src[m] = dq_s[place[m]]

    def send_dq(d, _):
        xd, yd, qd, cd = row_peer(d)
        remote(dq_src.at[cd], dq_out.at[:, own], dsem_s, dsem_r, r, cd).start()
        return 0

    lax.fori_loop(1, N_CP, send_dq, 0)
    dq_keep = pltpu.make_async_copy(dq_src.at[c], dq_out.at[:, own], lsem.at[2])
    dq_keep.start()

    keep.wait()
    for send in across:
        send.wait_recv()
    for k in range(4):
        shares[2 * k + 1].wait_recv()
        relays[k].wait_recv()

    w_mates = []

    def tile(start, gg):
        rows = pl.ds(pl.multiple_of(start, 256), 256)
        left, right = (kvbuf[2 * gg + i].reshape(512, 256) for i in range(2))
        return dot(xbuf[0, rows, :], left, 1, 0) + dot(xbuf[1, rows, :], right, 1, 0)

    for yo in range(2):
        for gg in range(2):
            w_src[yo * 256 : (yo + 1) * 256, gg * 256 : (gg + 1) * 256] = tile(
                (1 - q) * 512 + yo * 256, gg
            ).astype(BF16)
        rows = pl.ds(yo * 256, 256)
        w_mate = remote(w_src.at[rows], w_core.at[rows], wsem_s.at[yo], wsem_r.at[yo], r, mate)
        w_mate.start()
        w_mates.append(w_mate)
    for yo in range(2):
        for gg in range(2):
            w_own[yo * 256 : (yo + 1) * 256, gg * 256 : (gg + 1) * 256] = tile(q * 512 + yo * 256, gg)
    for yo in range(2):
        w_mates[yo].wait()
        rows = slice(yo * 256, (yo + 1) * 256)
        block = w_own[rows, :] + w_core[rows, :].astype(F32)
        wsend[:, :, yo] = block.astype(BF16).reshape(8, 2, 16, 512)

    for dz in FAR:
        zd = (z + dz) % 8
        remote(wsend.at[zd], wbuf.at[z], wsem_s.at[2], wsem_r.at[2], zd * 2 + low_y, c).start()
    wbuf[z] = wsend[z]
    take(wbuf.at[pl.ds(0, 7)], wsem_r.at[2])
    for yl in range(2):
        for yo in range(2):
            total = wbuf[0, yl, yo].astype(F32)
            for i in range(1, 8):
                total = total + wbuf[i, yl, yo].astype(F32)
            wsum[yl, yo] = total
    for dl, dy in ((0, 1), (1, 1), (1, 0)):
        yl, yo = (low_y + dl) % 2, (y + dy) % 2
        cd = x * 4 + yo * 2 + q
        remote(wsum.at[yl, yo], wpart.at[2 * low_y + y], wsem_s.at[3], wsem_r.at[3], z * 2 + yl, cd).start()
    wpart[2 * low_y + y] = wsum[low_y, y]
    take(wpart.at[pl.ds(0, 3)], wsem_r.at[3])
    for yy in range(2):
        total = wpart[yy] + wpart[2 + yy]
        for gg in range(2):
            j = 2 * yy + gg
            w_out[:, j * DH : (j + 1) * DH] = total[:, gg * 256 : gg * 256 + DH].astype(BF16)
            w_out[:, 512 + j * DH : 512 + (j + 1) * DH] = total[:, gg * 256 + DH : (gg + 1) * 256].astype(BF16)

    for send in to_mate + to_pair + shares + relays:
        send.wait_send()
    take(dq_src.at[pl.ds(0, N_CP - 1)], dsem_r)
    take(dq_src.at[pl.ds(0, N_CP - 1)], dsem_s)
    dq_keep.wait()
    for i, buf in enumerate((qbuf, kvbuf_in, gbuf, stbuf, tagbuf)):
        take(buf.at[pl.ds(0, N_CP - 1)], asem_s.at[i])
    for send in x_sends + across:
        send.wait_send()
    take(wbuf.at[pl.ds(0, 7)], wsem_s.at[2])
    take(wpart.at[pl.ds(0, 3)], wsem_s.at[3])


def shards(layer_input, queries, keys, values, outputs, out_grad, log_sum_exp, group_first, span_index, seq_length):
    cos_table, sin_table = rope_tables()
    anywhere = pl.BlockSpec(memory_space=pl.ANY)
    vmem = pl.BlockSpec(memory_space=pltpu.VMEM)
    smem = pl.BlockSpec(memory_space=pltpu.SMEM)
    dma = pltpu.SemaphoreType.DMA
    V = pltpu.VMEM
    scratch = [
        V((T, 4096), BF16), V((T, 2048), BF16), V((T, 2048), BF16), V((16, T, DH), F32), V((16, T, DH), F32),
        V((16, T, DH), BF16), V((16, T, DH), BF16), V((16, T, DH), BF16),
        V((16, 8, T), F32), V((16, 8, T), jnp.int32), V((16, 8, T), F32), V((8, T), jnp.int32),
        pltpu.SMEM((16, 8, T), jnp.int32), pltpu.SMEM((16,), jnp.int32),
        V((16, T, DH), BF16), V((16, T, DH), BF16), V((2, 16, T, DH), BF16),
        V((NB, DH, BL), BF16), V((NB, 8, BL), F32), V((NB, DH, BL), F32), V((16, T, 256), BF16),
        V((4, 1024, T), BF16), V((2, 1024, 512), BF16), V((2, 4, T, 256), BF16), V((2, 4, T, 256), BF16),
        V((4, T, 256), BF16), V((4, T, 256), BF16), V((4, 4, T, 256), BF16),
        V((16, T, DH), BF16), V((16, T, DH), BF16), V((512, 512), BF16), V((512, 512), BF16), V((512, 512), F32),
        V((8, 2, 2, 16, 512), BF16), V((8, 2, 2, 16, 512), BF16), V((2, 2, 16, 512), F32), V((4, 16, 512), F32),
        dma((11,)), dma((5,)), dma((5,)), dma((7,)), dma((7,)), dma((6, 4)), dma((6, 4)), dma((4,)), dma((4,)), dma, dma,
    ]
    return pl.pallas_call(
        kernel,
        out_shape=(
            jax.ShapeDtypeStruct((T, 2048), BF16),
            jax.ShapeDtypeStruct((16, 1024), BF16),
        ),
        in_specs=[anywhere] * 6 + [vmem, smem, smem, smem, anywhere, anywhere],
        out_specs=(anywhere, vmem),
        scratch_shapes=scratch,
        compiler_params=pltpu.CompilerParams(
            collective_id=0, has_side_effects=True, vmem_limit_bytes=62 * 1024 * 1024
        ),
        name="attention_backward",
    )(
        layer_input, queries, keys, values, outputs, out_grad, log_sum_exp,
        group_first, span_index, seq_length, jnp.asarray(cos_table), jnp.asarray(sin_table),
    )


def solution(mesh):
    both = P(("dp", "cp"), None)
    placed = (both,) * 7 + (P("dp", "cp"),) * 3
    return jax.shard_map(shards, mesh=mesh, in_specs=placed, out_specs=(both, both), check_vma=False)
```

time: 126 us -> 95.7 us (0.76)
  Pallas kernels: 112 us -> 89 us
  local copies, waits for them, and re-layouts: 10.8 us -> 3.93 us
    pallas_call x1, Pallas kernels: 112 us -> 89 us  [shards(): pl.pallas_call(kernel, out_shape=(jax.ShapeDtypeStruct((T, 2048), BF16),...]
    unnamed x19 -> x5, local copies, waits for them, and re-layouts: 10.8 us -> 3.93 us
where the time goes in v2:
time: 95.7 us; the launch traced here: 95.5 us
  Pallas kernels  89 us (93%)
  local copies, waits for them, and re-layouts  3.93 us (4%)
  between operations  2.59 us (3%)
    pallas_call x1, Pallas kernels, shards(): pl.pallas_call(kernel, out_shape=(jax.ShapeDtypeStruct((T, 2048), BF16),...  89 us
    unnamed x5, local copies, waits for them, and re-layouts  3.93 us

profile of v2, /device:TPU:1, one launch (start us, length us, event | category | flops | bytes accessed | tf_op | source)
XLA Modules:
  0.0 95.5 jit_solution(5869812847541440966)
XLA Ops:
  2.6 1.4 %copy.14.lse_ref = f32[128,16]{1,0:T(8,128)} copy(f32[128,16]{0,1:T(8,128)} %param.18) | data formatting | bytes 16384 | tf_op args[6]
  4.0 89.0 %attention_backward.1 = (bf16[128,2048]{1,0:T(8,128)(2,1)}, bf16[16,1024]{1,0:T(8,128)(2,1)}) custom-call(bf16[128,4096]{1,0:T(8,128)(2,1)} %x_hbm.1, bf16[128,2048]{1,0:T(8,128)(2,1)} %q_hbm.1, bf16[128,512]{1,0:T(8,128)(2,1)} %k_hbm.1, bf16[128,512]{1,0:T(8,128)(2,1)} %v_hbm.1, bf16[128,2048]{1,0:T(8,128)(2,1)} %o_hbm.1, bf16[128,2048]{1,0:T(8,128)(2,1)} %g_hbm.1, ...), custom_call_target="tpu_custom_call" | custom-call | tf_op jit(solution)/shard_map/attention_backward/pallas_call | solution.py:416
  93.0 0.0 copy-start
  93.0 1.9 %copy.20 = bf16[128,2048]{1,0:T(8,128)(2,1)} copy(bf16[128,2048]{1,0:T(8,128)(2,1)} %get-tuple-element.4) | data formatting | bytes 1048576
  94.9 0.0 copy-done
  94.9 0.6 copy.21
Async XLA Ops:
  93.0 1.9 %copy-start = (bf16[16,1024]{1,0:T(8,128)(2,1)S(1)}, bf16[16,1024]{1,0:T(8,128)(2,1)}, u32[]{:S(2)}) copy-start(bf16[16,1024]{1,0:T(8,128)(2,1)} %get-tuple-element.5) | copy-start | bytes 98308

commit v3 on v2

--- a/solution.py
+++ b/solution.py
@@ -46,8 +46,8 @@
     x_v, o_v, g_v, cos_v, sin_v,
     qbuf, gbuf, kvbuf_in, stbuf, tagbuf, st_src, tag_src, tags_s, sig_s,
     qs, gs, kvs, kts, st_s, dqt, dkv_s,
-    xts, xbuf, core_src, core_buf, rs_src, rs_buf, kvbuf,
-    dq_s, dq_src, w_src, w_core, w_own, wsend, wbuf, wsum, wpart,
+    pbuf, xts, xbuf, core_src, core_buf, pair_src, pair_buf, kvbuf,
+    dq_s, dq_src, w_src, w_core, w_own, ysend, ybuf, zsend, zbuf,
     lsem, asem_s, asem_r, xsem_s, xsem_r, ksem_s, ksem_r, wsem_s, wsem_r, dsem_s, dsem_r,
 ):
     r = lax.axis_index("dp")
@@ -163,7 +163,7 @@
             block = x_v[:, pl.ds(pl.multiple_of(b * 256 + part * 128, 128), 128)].T
             for k in range(8):
                 owner = part * 8 + k
-                start = (owner % 2) * 512 + ((owner // 2) % 2) * 256 + b * 16
+                start = (owner % 2) * 512 + (b % 2) * 256 + ((owner // 2) % 2) * 128 + (b // 2) * 16
                 xts[owner // 4, pl.ds(pl.multiple_of(start, 16), 16), :] = block[k * 16 : (k + 1) * 16]
         return 0
 
@@ -195,14 +195,14 @@
         take(buf.at[pl.ds(0, N_CP - 1)], asem_r.at[i])
 
     def x_slot(xs, ys):
-        lanes = pl.ds(pl.multiple_of(((xs % 2) * 2 + ys) * T, T), T)
-        return xbuf.at[xs // 2, :, lanes]
-
-    x_sends = []
-    for i, d in enumerate((1, 3, 2)):
-        send = remote(xts.at[(x + d) % 4], x_slot(x, y), xsem_s.at[i], xsem_r.at[i], r, ((x + d) % 4) * 4 + y * 2 + q)
-        send.start()
-        x_sends.append(send)
+        return xbuf.at[:, pl.ds(pl.multiple_of((xs * 2 + ys) * T, T), T)]
+
+    x_sends = [
+        remote(xts.at[(x + d) % 4], x_slot(x, y), xsem_s.at[i], xsem_r.at[i], r, ((x + d) % 4) * 4 + y * 2 + q)
+        for i, d in enumerate((1, 3, 2))
+    ]
+    x_sends[0].start()
+    x_sends[1].start()
     keep = pltpu.make_async_copy(xts.at[x], x_slot(x, y), lsem.at[0])
     keep.start()
     across = [remote(xts.at[x], x_slot(x, y), xsem_s.at[3], xsem_r.at[3], r, y_mate)]
@@ -223,92 +223,106 @@
         kts[p // NT, :, (p % NT) * T : (p % NT + 1) * T] = kvs[0, p].T
     dqt[...] = jnp.zeros_like(dqt)
 
-    def key_block(step, _):
+    g, u = x // 2, x % 2
+    pair_dev, other_dev = (x + 1 - 2 * u) * 4 + y * 2 + q, (3 - x) * 4 + y * 2 + q
+    chunks = [pl.ds(k * 2 * T, 2 * T) for k in range(4)]
+    to_mate, to_pair, to_other = {}, {}, {}
+
+    def sum_mate(part):
+        for k in range(4):
+            for i in range(2):
+                e = 2 * k + i
+                core_src[part, pl.ds(e * T, T), :] = dkv_s[part, tags_s[2 * e + (1 - q), 0, 0]]
+            to_mate[part, k] = remote(
+                core_src.at[part, chunks[k]], core_buf.at[part, chunks[k]],
+                ksem_s.at[0, part, k], ksem_r.at[0, part, k], r, mate,
+            )
+            to_mate[part, k].start()
+
+    def chip_sum(part, k):
+        own_part = [dkv_s[part, tags_s[2 * (2 * k + i) + q, 0, 0]].astype(F32) for i in range(2)]
+        return jnp.concatenate(own_part, axis=0) + core_buf[part, chunks[k], :].astype(F32)
+
+    def sum_pair(part):
+        for k in range(4):
+            to_mate[part, k].wait_recv()
+            pair_src[part, chunks[k], :] = chip_sum(part, k).astype(BF16)
+            to_pair[part, k] = remote(
+                pair_src.at[part, chunks[k]], pair_buf.at[part, chunks[k]],
+                ksem_s.at[1, part, k], ksem_r.at[1, part, k], r, pair_dev,
+            )
+            to_pair[part, k].start()
+
+    def share(part):
+        for k in range(4):
+            to_pair[part, k].wait_recv()
+            lanes = pl.ds(pl.multiple_of(g * DH, DH), DH)
+            total = chip_sum(part, k) + pair_buf[part, chunks[k], :].astype(F32)
+            kvbuf[part, chunks[k], lanes] = total.astype(BF16)
+            done = kvbuf.at[part, chunks[k], lanes]
+            to_other[part, k] = remote(
+                done, done, ksem_s.at[2, part, k], ksem_r.at[2, part, k], r, other_dev
+            )
+            to_other[part, k].start()
+
+    def value_block(step, _):
         kb = NB - 1 - step
         key = kvs[0, pl.ds(NT * kb, NT)].reshape(BL, DH)
-        value = kvs[1, pl.ds(NT * kb, NT)].reshape(BL, DH)
-        key_t = kts[kb]
-
-        def unit(qb, carry, diagonal):
-            dk, dv = carry
+
+        def unit(qb, dv, diagonal):
             query = qs[pl.ds(NT * qb, NT)].reshape(BL, DH)
             grad = gs[pl.ds(NT * qb, NT)].reshape(BL, DH)
             stats = st_s[qb]
             scores = dot(key, query, 1, 1)
-            dp = dot(value, grad, 1, 1)
             s_at = lax.broadcasted_iota(jnp.int32, (BL, BL), 0)
             allowed = s_at >= stats[2:3].astype(jnp.int32) - kb * BL
             if diagonal:
                 allowed = allowed & (s_at <= lax.broadcasted_iota(jnp.int32, (BL, BL), 1))
             probs = jnp.where(allowed, jnp.exp2(scores * (SCALE * LOG2E) - stats[0:1]), 0.0)
-            ds = (probs * (dp - stats[1:2])).astype(BF16)
-            dv = dv + dot(probs.astype(BF16), grad, 1, 0)
-            dk = dk + dot(ds, query, 1, 0)
+            pbuf[kb * NB + qb] = probs
+            return dv + dot(probs.astype(BF16), grad, 1, 0)
+
+        dv = unit(kb, jnp.zeros((BL, DH), F32), True)
+        dv = lax.fori_loop(kb + 1, NB, lambda qb, t: unit(qb, t, False), dv)
+        for i in range(NT):
+            dkv_s[0, NT * kb + i] = dv[i * T : (i + 1) * T].astype(BF16)
+        return 0
+
+    def key_block(step, _):
+        kb = NB - 1 - step
+        value = kvs[1, pl.ds(NT * kb, NT)].reshape(BL, DH)
+        key_t = kts[kb]
+
+        def unit(qb, dk):
+            query = qs[pl.ds(NT * qb, NT)].reshape(BL, DH)
+            grad = gs[pl.ds(NT * qb, NT)].reshape(BL, DH)
+            dp = dot(value, grad, 1, 1)
+            ds = (pbuf[kb * NB + qb] * (dp - st_s[qb][1:2])).astype(BF16)
             dqt[qb] += dot(key_t, ds, 1, 0)
-            return dk, dv
-
-        zero = jnp.zeros((BL, DH), F32)
-        carry = unit(kb, (zero, zero), True)
-        dk, dv = lax.fori_loop(kb + 1, NB, lambda qb, cc: unit(qb, cc, False), carry)
+            return dk + dot(ds, query, 1, 0)
+
+        dk = lax.fori_loop(kb, NB, unit, jnp.zeros((BL, DH), F32))
         for i in range(NT):
             p = NT * kb + i
-            rows = slice(i * T, (i + 1) * T)
-            turned = dk[rows] * SCALE
+            turned = dk[i * T : (i + 1) * T] * SCALE
             sig = sig_s[p]
             plain = turned * cos_v[sig] + pltpu.roll(turned, DH // 2, 1) * sin_v[sig]
-            dkv_s[p] = jnp.concatenate([plain, dv[rows]], axis=1).astype(BF16)
+            dkv_s[1, p] = plain.astype(BF16)
         return 0
 
-    lax.fori_loop(0, NB - 1, key_block, 0)
+    lax.fori_loop(0, NB, value_block, 0)
+    sum_mate(0)
+    x_sends[2].start()
+    lax.fori_loop(0, 2, key_block, 0)
     hand_on(0)
     hand_on(1)
-    lax.fori_loop(NB - 1, NB, key_block, 0)
-
-    u = x % 2
-    pair, other = x + 1 - 2 * u, 3 - x
-    pair_dev, other_dev = pair * 4 + y * 2 + q, other * 4 + y * 2 + q
-
-    def k_copy(src, dst, i, k, dev):
-        return remote(src, dst, ksem_s.at[i, k], ksem_r.at[i, k], r, dev)
-
-    to_mate = []
-    for i, half in enumerate((1 - u, u)):
-        for k in range(4):
-            e = 4 * half + k
-            core_src[i, k] = dkv_s[tags_s[2 * e + (1 - q), 0, 0]]
-            to_mate.append(k_copy(core_src.at[i, k], core_buf.at[i, k], i, k, mate))
-            to_mate[-1].start()
-
-    def chip_sum(i, k):
-        e = 4 * (1 - u if i == 0 else u) + k
-        return dkv_s[tags_s[2 * e + q, 0, 0]].astype(F32) + core_buf[i, k].astype(F32)
-
-    to_pair = []
-    for k in range(4):
-        to_mate[k].wait_recv()
-        rs_src[k] = chip_sum(0, k).astype(BF16)
-        to_pair.append(k_copy(rs_src.at[k], rs_buf.at[k], 2, k, pair_dev))
-        to_pair[-1].start()
+    sum_pair(0)
+    lax.fori_loop(2, NB, key_block, 0)
+    sum_mate(1)
     hand_on(2)
-
-    shares, relays = [], []
-
-    def relay(k):
-        shares[2 * k].wait_recv()
-        relays.append(k_copy(kvbuf.at[pair, k], kvbuf.at[pair, k], 5, k, other_dev))
-        relays[-1].start()
-
-    for k in range(4):
-        to_mate[4 + k].wait_recv()
-        mine = chip_sum(1, k)
-        to_pair[k].wait_recv()
-        kvbuf[x, k] = (mine + rs_buf[k].astype(F32)).astype(BF16)
-        for i, dev in ((3, pair_dev), (4, other_dev)):
-            shares.append(k_copy(kvbuf.at[x, k], kvbuf.at[x, k], i, k, dev))
-            shares[-1].start()
-        if k:
-            relay(k - 1)
-    relay(3)
+    share(0)
+    sum_pair(1)
+    share(1)
 
     for p in range(N_CP):
         dq_s[p] = (dqt[p // NT, :, (p % NT) * T : (p % NT + 1) * T] * SCALE).T.astype(BF16)
@@ -320,68 +334,75 @@
         remote(dq_src.at[cd], dq_out.at[:, own], dsem_s, dsem_r, r, cd).start()
         return 0
 
+    keep.wait()
+    for send in across:
+        send.wait_recv()
+
+    def tile(start, part):
+        return dot(xbuf[pl.ds(pl.multiple_of(start, 512), 512), :], kvbuf[part], 1, 0).reshape(4, 128, 256)
+
+    def tile_mate(part):
+        for k in range(4):
+            to_other[part, k].wait_recv()
+        w_src[part] = tile((1 - q) * 512, part).astype(BF16)
+        w_mates[part] = remote(w_src.at[part], w_core.at[part], wsem_s.at[0, part], wsem_r.at[0, part], r, mate)
+        w_mates[part].start()
+
+    def tile_own(part):
+        w_own[part] = tile(q * 512, part)
+
+    def send_y(part):
+        w_mates[part].wait_recv()
+        total = w_own[part] + w_core[part].astype(F32)
+        w_own[part] = total
+        ysend[part] = total.astype(BF16)
+        for dl, dy in ((0, 1), (1, 1), (1, 0)):
+            yl, yo = (low_y + dl) % 2, (y + dy) % 2
+            remote(
+                ysend.at[part, 2 * yl + yo], ybuf.at[part, 2 * low_y + y],
+                wsem_s.at[1, part], wsem_r.at[1, part], z * 2 + yl, x * 4 + yo * 2 + q,
+            ).start()
+
+    def send_z(part):
+        take(ybuf.at[part, pl.ds(0, 3)], wsem_r.at[1, part])
+        near = w_own[part, 2 * low_y + y] + ybuf[part, 2 * (1 - low_y) + y].astype(F32)
+        far = ybuf[part, 1 - y].astype(F32) + ybuf[part, 3 - y].astype(F32)
+        zsend[part, :, y] = near.astype(BF16).reshape(8, 16, 256)
+        zsend[part, :, 1 - y] = far.astype(BF16).reshape(8, 16, 256)
+        for dz in FAR:
+            zd = (z + dz) % 8
+            remote(
+                zsend.at[part, zd], zbuf.at[part, z], wsem_s.at[2, part], wsem_r.at[2, part], zd * 2 + low_y, c
+            ).start()
+        zbuf[part, z] = zsend[part, z]
+
+    def finish(part):
+        take(zbuf.at[part, pl.ds(0, 7)], wsem_r.at[2, part])
+        total = zbuf[part, 0].astype(F32)
+        for i in range(1, 8):
+            total = total + zbuf[part, i].astype(F32)
+        for yy in range(2):
+            start = 512 * (1 - part) + 256 * yy
+            w_out[:, start : start + 256] = total[yy].astype(BF16)
+
+    w_mates = {}
+    tile_mate(0)
+    tile_own(0)
+    tile_mate(1)
+    send_y(0)
+    tile_own(1)
+    send_y(1)
+    send_z(0)
     lax.fori_loop(1, N_CP, send_dq, 0)
     dq_keep = pltpu.make_async_copy(dq_src.at[c], dq_out.at[:, own], lsem.at[2])
     dq_keep.start()
-
-    keep.wait()
-    for send in across:
-        send.wait_recv()
-    for k in range(4):
-        shares[2 * k + 1].wait_recv()
-        relays[k].wait_recv()
-
-    w_mates = []
-
-    def tile(start, gg):
-        rows = pl.ds(pl.multiple_of(start, 256), 256)
-        left, right = (kvbuf[2 * gg + i].reshape(512, 256) for i in range(2))
-        return dot(xbuf[0, rows, :], left, 1, 0) + dot(xbuf[1, rows, :], right, 1, 0)
-
-    for yo in range(2):
-        for gg in range(2):
-            w_src[yo * 256 : (yo + 1) * 256, gg * 256 : (gg + 1) * 256] = tile(
-                (1 - q) * 512 + yo * 256, gg
-            ).astype(BF16)
-        rows = pl.ds(yo * 256, 256)
-        w_mate = remote(w_src.at[rows], w_core.at[rows], wsem_s.at[yo], wsem_r.at[yo], r, mate)
-        w_mate.start()
-        w_mates.append(w_mate)
-    for yo in range(2):
-        for gg in range(2):
-            w_own[yo * 256 : (yo + 1) * 256, gg * 256 : (gg + 1) * 256] = tile(q * 512 + yo * 256, gg)
-    for yo in range(2):
-        w_mates[yo].wait()
-        rows = slice(yo * 256, (yo + 1) * 256)
-        block = w_own[rows, :] + w_core[rows, :].astype(F32)
-        wsend[:, :, yo] = block.astype(BF16).reshape(8, 2, 16, 512)
-
-    for dz in FAR:
-        zd = (z + dz) % 8
-        remote(wsend.at[zd], wbuf.at[z], wsem_s.at[2], wsem_r.at[2], zd * 2 + low_y, c).start()
-    wbuf[z] = wsend[z]
-    take(wbuf.at[pl.ds(0, 7)], wsem_r.at[2])
-    for yl in range(2):
-        for yo in range(2):
-            total = wbuf[0, yl, yo].astype(F32)
-            for i in range(1, 8):
-                total = total + wbuf[i, yl, yo].astype(F32)
-            wsum[yl, yo] = total
-    for dl, dy in ((0, 1), (1, 1), (1, 0)):
-        yl, yo = (low_y + dl) % 2, (y + dy) % 2
-        cd = x * 4 + yo * 2 + q
-        remote(wsum.at[yl, yo], wpart.at[2 * low_y + y], wsem_s.at[3], wsem_r.at[3], z * 2 + yl, cd).start()
-    wpart[2 * low_y + y] = wsum[low_y, y]
-    take(wpart.at[pl.ds(0, 3)], wsem_r.at[3])
-    for yy in range(2):
-        total = wpart[yy] + wpart[2 + yy]
-        for gg in range(2):
-            j = 2 * yy + gg
-            w_out[:, j * DH : (j + 1) * DH] = total[:, gg * 256 : gg * 256 + DH].astype(BF16)
-            w_out[:, 512 + j * DH : 512 + (j + 1) * DH] = total[:, gg * 256 + DH : (gg + 1) * 256].astype(BF16)
-
-    for send in to_mate + to_pair + shares + relays:
-        send.wait_send()
+    send_z(1)
+    finish(0)
+    finish(1)
+
+    for sends in (to_mate, to_pair, to_other):
+        for send in sends.values():
+            send.wait_send()
     take(dq_src.at[pl.ds(0, N_CP - 1)], dsem_r)
     take(dq_src.at[pl.ds(0, N_CP - 1)], dsem_s)
     dq_keep.wait()
@@ -389,8 +410,10 @@
         take(buf.at[pl.ds(0, N_CP - 1)], asem_s.at[i])
     for send in x_sends + across:
         send.wait_send()
-    take(wbuf.at[pl.ds(0, 7)], wsem_s.at[2])
-    take(wpart.at[pl.ds(0, 3)], wsem_s.at[3])
+    for part in range(2):
+        w_mates[part].wait_send()
+        take(ybuf.at[part, pl.ds(0, 3)], wsem_s.at[1, part])
+        take(zbuf.at[part, pl.ds(0, 7)], wsem_s.at[2, part])
 
 
 def shards(layer_input, queries, keys, values, outputs, out_grad, log_sum_exp, group_first, span_index, seq_length):
@@ -406,12 +429,13 @@
         V((16, 8, T), F32), V((16, 8, T), jnp.int32), V((16, 8, T), F32), V((8, T), jnp.int32),
         pltpu.SMEM((16, 8, T), jnp.int32), pltpu.SMEM((16,), jnp.int32),
         V((16, T, DH), BF16), V((16, T, DH), BF16), V((2, 16, T, DH), BF16),
-        V((NB, DH, BL), BF16), V((NB, 8, BL), F32), V((NB, DH, BL), F32), V((16, T, 256), BF16),
-        V((4, 1024, T), BF16), V((2, 1024, 512), BF16), V((2, 4, T, 256), BF16), V((2, 4, T, 256), BF16),
-        V((4, T, 256), BF16), V((4, T, 256), BF16), V((4, 4, T, 256), BF16),
-        V((16, T, DH), BF16), V((16, T, DH), BF16), V((512, 512), BF16), V((512, 512), BF16), V((512, 512), F32),
-        V((8, 2, 2, 16, 512), BF16), V((8, 2, 2, 16, 512), BF16), V((2, 2, 16, 512), F32), V((4, 16, 512), F32),
-        dma((11,)), dma((5,)), dma((5,)), dma((7,)), dma((7,)), dma((6, 4)), dma((6, 4)), dma((4,)), dma((4,)), dma, dma,
+        V((NB, DH, BL), BF16), V((NB, 8, BL), F32), V((NB, DH, BL), F32), V((2, 16, T, DH), BF16),
+        V((NB * NB, BL, BL), F32), V((4, 1024, T), BF16), V((1024, 1024), BF16), V((2, 1024, DH), BF16),
+        V((2, 1024, DH), BF16), V((2, 1024, DH), BF16), V((2, 1024, DH), BF16), V((2, 1024, 256), BF16),
+        V((16, T, DH), BF16), V((16, T, DH), BF16), V((2, 4, T, 256), BF16), V((2, 4, T, 256), BF16),
+        V((2, 4, T, 256), F32), V((2, 4, T, 256), BF16), V((2, 4, T, 256), BF16),
+        V((2, 8, 2, 16, 256), BF16), V((2, 8, 2, 16, 256), BF16),
+        dma((11,)), dma((5,)), dma((5,)), dma((7,)), dma((7,)), dma((3, 2, 4)), dma((3, 2, 4)), dma((3, 2)), dma((3, 2)), dma, dma,
     ]
     return pl.pallas_call(
         kernel,

time: 95.7 us -> 87.6 us (0.915)
  the two profiles are of different devices: /device:TPU:1 before, /device:TPU:32 now
where the time goes in v3:
time: 87.6 us; the launch traced here: 87.4 us
  Pallas kernels  80.9 us (92%)
  local copies, waits for them, and re-layouts  3.93 us (4%)
  between operations  2.59 us (3%)
    pallas_call x1, Pallas kernels, shards(): pl.pallas_call(kernel, out_shape=(jax.ShapeDtypeStruct((T, 2048), BF16),...  80.9 us
    unnamed x5, local copies, waits for them, and re-layouts  3.93 us

profile of v3, /device:TPU:32, one launch (start us, length us, event | category | flops | bytes accessed | tf_op | source)
XLA Modules:
  0.0 87.4 jit_solution(10041744451371254559)
XLA Ops:
  2.6 1.4 %copy.14.lse_ref = f32[128,16]{1,0:T(8,128)} copy(f32[128,16]{0,1:T(8,128)} %param.18) | data formatting | bytes 16384 | tf_op args[6]
  4.0 80.9 %attention_backward.1 = (bf16[128,2048]{1,0:T(8,128)(2,1)}, bf16[16,1024]{1,0:T(8,128)(2,1)}) custom-call(bf16[128,4096]{1,0:T(8,128)(2,1)} %x_hbm.1, bf16[128,2048]{1,0:T(8,128)(2,1)} %q_hbm.1, bf16[128,512]{1,0:T(8,128)(2,1)} %k_hbm.1, bf16[128,512]{1,0:T(8,128)(2,1)} %v_hbm.1, bf16[128,2048]{1,0:T(8,128)(2,1)} %o_hbm.1, bf16[128,2048]{1,0:T(8,128)(2,1)} %g_hbm.1, ...), custom_call_target="tpu_custom_call" | custom-call | tf_op jit(solution)/shard_map/attention_backward/pallas_call | solution.py:440
  84.9 0.0 copy-start
  84.9 1.9 %copy.20 = bf16[128,2048]{1,0:T(8,128)(2,1)} copy(bf16[128,2048]{1,0:T(8,128)(2,1)} %get-tuple-element.4) | data formatting | bytes 1048576
  86.8 0.0 copy-done
  86.8 0.6 copy.21
Async XLA Ops:
  84.9 1.9 %copy-start = (bf16[16,1024]{1,0:T(8,128)(2,1)S(1)}, bf16[16,1024]{1,0:T(8,128)(2,1)}, u32[]{:S(2)}) copy-start(bf16[16,1024]{1,0:T(8,128)(2,1)} %get-tuple-element.5) | copy-start | bytes 98308

commit v4 on v3

--- a/solution.py
+++ b/solution.py
@@ -41,9 +41,9 @@
 
 
 def kernel(
-    x_hbm, q_hbm, k_hbm, v_hbm, o_hbm, g_hbm, lse_ref, first_ref, span_ref, length_ref, cos_hbm, sin_hbm,
+    x_hbm, q_hbm, k_hbm, v_hbm, o_hbm, g_hbm, lse_hbm, first_ref, span_ref, length_ref, cos_hbm, sin_hbm,
     dq_out, w_out,
-    x_v, o_v, g_v, cos_v, sin_v,
+    x_v, o_v, g_v, lse_v, cos_v, sin_v,
     qbuf, gbuf, kvbuf_in, stbuf, tagbuf, st_src, tag_src, tags_s, sig_s,
     qs, gs, kvs, kts, st_s, dqt, dkv_s,
     pbuf, xts, xbuf, core_src, core_buf, pair_src, pair_buf, kvbuf,
@@ -64,12 +64,12 @@
     def greet(rd, cd):
         pl.semaphore_signal(barrier, inc=1, device_id=(rd, cd), device_id_type=MESH)
 
-    for d in range(1, N_CP):
-        greet(r, (c + d) % N_CP)
     for dz in FAR:
         greet(((z + dz) % 8) * 2 + low_y, c)
     greet(beside, c)
     greet(beside, y_mate)
+    for d in range(1, N_CP):
+        greet(r, (c + d) % N_CP)
 
     own = pl.ds(head * DH, DH)
     own_kv = pl.ds((head // 4) * DH, DH)
@@ -77,6 +77,7 @@
     loads = [
         pltpu.make_async_copy(o_hbm, o_v, lsem.at[0]),
         pltpu.make_async_copy(g_hbm, g_v, lsem.at[1]),
+        pltpu.make_async_copy(lse_hbm, lse_v, lsem.at[11]),
         pltpu.make_async_copy(x_hbm, x_v, lsem.at[2]),
         pltpu.make_async_copy(cos_hbm, cos_v, lsem.at[3]),
         pltpu.make_async_copy(sin_hbm, sin_v, lsem.at[4]),
@@ -131,9 +132,9 @@
 
     pos = span * T + lax.broadcasted_iota(jnp.int32, (1, T), 1)
     low = jnp.where(pos < length, first * T, 2 * N_CP * T).astype(F32)
-    lse_t = jnp.concatenate([lse_ref[...] * LOG2E, jnp.zeros((T, T - 16), F32)], axis=1).T
-    for load in loads[:2]:
+    for load in loads[:3]:
         load.wait()
+    lse_t = jnp.concatenate([lse_v[...] * LOG2E, jnp.zeros((T, T - 16), F32)], axis=1).T
     lane = lax.broadcasted_iota(jnp.int32, (T, T), 1)
     delta = jnp.zeros((T, T), F32)
     for h in range(16):
@@ -156,7 +157,7 @@
     stbuf[c] = st_src[head]
     tagbuf[c] = tag_src[...]
 
-    loads[2].wait()
+    loads[3].wait()
 
     def turn_x(b, _):
         for part in range(2):
@@ -189,10 +190,38 @@
     forward = remote(kvs.at[q], kvs.at[q], lsem.at[9], lsem.at[10], r, mate)
     forward.start()
 
-    for load in loads[3:]:
+    for load in loads[4:7]:
         load.wait()
-    for i, buf in ((0, qbuf), (2, gbuf), (3, stbuf)):
-        take(buf.at[pl.ds(0, N_CP - 1)], asem_r.at[i])
+    take(qbuf.at[pl.ds(0, N_CP - 1)], asem_r.at[0])
+    take(stbuf.at[pl.ds(0, N_CP - 1)], asem_r.at[3])
+    for p in range(N_CP):
+        qs[p] = qbuf[member[p]]
+        st_s[p // NT, :, (p % NT) * T : (p % NT + 1) * T] = stbuf[member[p]]
+    forward.wait()
+    for p in range(N_CP):
+        kts[p // NT, :, (p % NT) * T : (p % NT + 1) * T] = kvs[0, p].T
+    dqt[...] = jnp.zeros_like(dqt)
+
+    def prob_block(kb, _):
+        key = kvs[0, pl.ds(NT * kb, NT)].reshape(BL, DH)
+
+        def unit(qb, diagonal):
+            query = qs[pl.ds(NT * qb, NT)].reshape(BL, DH)
+            stats = st_s[qb]
+            scores = dot(key, query, 1, 1)
+            s_at = lax.broadcasted_iota(jnp.int32, (BL, BL), 0)
+            allowed = s_at >= stats[2:3].astype(jnp.int32) - kb * BL
+            if diagonal:
+                allowed = allowed & (s_at <= lax.broadcasted_iota(jnp.int32, (BL, BL), 1))
+            pbuf[kb * NB + qb] = jnp.where(allowed, jnp.exp2(scores * (SCALE * LOG2E) - stats[0:1]), 0.0)
+            return 0
+
+        unit(kb, True)
+        return lax.fori_loop(kb + 1, NB, lambda qb, t: unit(qb, False), 0)
+
+    lax.fori_loop(0, NB, prob_block, 0)
+    loads[7].wait()
+    take(gbuf.at[pl.ds(0, N_CP - 1)], asem_r.at[2])
 
     def x_slot(xs, ys):
         return xbuf.at[:, pl.ds(pl.multiple_of((xs * 2 + ys) * T, T), T)]
@@ -201,8 +230,8 @@
         remote(xts.at[(x + d) % 4], x_slot(x, y), xsem_s.at[i], xsem_r.at[i], r, ((x + d) % 4) * 4 + y * 2 + q)
         for i, d in enumerate((1, 3, 2))
     ]
-    x_sends[0].start()
-    x_sends[1].start()
+    for send in x_sends:
+        send.start()
     keep = pltpu.make_async_copy(xts.at[x], x_slot(x, y), lsem.at[0])
     keep.start()
     across = [remote(xts.at[x], x_slot(x, y), xsem_s.at[3], xsem_r.at[3], r, y_mate)]
@@ -215,13 +244,7 @@
         across[-1].start()
 
     for p in range(N_CP):
-        qs[p] = qbuf[member[p]]
         gs[p] = gbuf[member[p]]
-        st_s[p // NT, :, (p % NT) * T : (p % NT + 1) * T] = stbuf[member[p]]
-    forward.wait()
-    for p in range(N_CP):
-        kts[p // NT, :, (p % NT) * T : (p % NT + 1) * T] = kvs[0, p].T
-    dqt[...] = jnp.zeros_like(dqt)
 
     g, u = x // 2, x % 2
     pair_dev, other_dev = (x + 1 - 2 * u) * 4 + y * 2 + q, (3 - x) * 4 + y * 2 + q
@@ -265,25 +288,12 @@
             )
             to_other[part, k].start()
 
-    def value_block(step, _):
-        kb = NB - 1 - step
-        key = kvs[0, pl.ds(NT * kb, NT)].reshape(BL, DH)
-
-        def unit(qb, dv, diagonal):
-            query = qs[pl.ds(NT * qb, NT)].reshape(BL, DH)
+    def value_block(kb, _):
+        def unit(qb, dv):
             grad = gs[pl.ds(NT * qb, NT)].reshape(BL, DH)
-            stats = st_s[qb]
-            scores = dot(key, query, 1, 1)
-            s_at = lax.broadcasted_iota(jnp.int32, (BL, BL), 0)
-            allowed = s_at >= stats[2:3].astype(jnp.int32) - kb * BL
-            if diagonal:
-                allowed = allowed & (s_at <= lax.broadcasted_iota(jnp.int32, (BL, BL), 1))
-            probs = jnp.where(allowed, jnp.exp2(scores * (SCALE * LOG2E) - stats[0:1]), 0.0)
-            pbuf[kb * NB + qb] = probs
-            return dv + dot(probs.astype(BF16), grad, 1, 0)
-
-        dv = unit(kb, jnp.zeros((BL, DH), F32), True)
-        dv = lax.fori_loop(kb + 1, NB, lambda qb, t: unit(qb, t, False), dv)
+            return dv + dot(pbuf[kb * NB + qb].astype(BF16), grad, 1, 0)
+
+        dv = lax.fori_loop(kb, NB, unit, jnp.zeros((BL, DH), F32))
         for i in range(NT):
             dkv_s[0, NT * kb + i] = dv[i * T : (i + 1) * T].astype(BF16)
         return 0
@@ -312,16 +322,16 @@
 
     lax.fori_loop(0, NB, value_block, 0)
     sum_mate(0)
-    x_sends[2].start()
     lax.fori_loop(0, 2, key_block, 0)
+    sum_pair(0)
+    lax.fori_loop(2, 3, key_block, 0)
     hand_on(0)
     hand_on(1)
-    sum_pair(0)
-    lax.fori_loop(2, NB, key_block, 0)
+    lax.fori_loop(3, NB, key_block, 0)
     sum_mate(1)
-    hand_on(2)
     share(0)
     sum_pair(1)
+    hand_on(2)
     share(1)
 
     for p in range(N_CP):
@@ -424,7 +434,7 @@
     dma = pltpu.SemaphoreType.DMA
     V = pltpu.VMEM
     scratch = [
-        V((T, 4096), BF16), V((T, 2048), BF16), V((T, 2048), BF16), V((16, T, DH), F32), V((16, T, DH), F32),
+        V((T, 4096), BF16), V((T, 2048), BF16), V((T, 2048), BF16), V((T, 16), F32), V((16, T, DH), F32), V((16, T, DH), F32),
         V((16, T, DH), BF16), V((16, T, DH), BF16), V((16, T, DH), BF16),
         V((16, 8, T), F32), V((16, 8, T), jnp.int32), V((16, 8, T), F32), V((8, T), jnp.int32),
         pltpu.SMEM((16, 8, T), jnp.int32), pltpu.SMEM((16,), jnp.int32),
@@ -435,7 +445,7 @@
         V((16, T, DH), BF16), V((16, T, DH), BF16), V((2, 4, T, 256), BF16), V((2, 4, T, 256), BF16),
         V((2, 4, T, 256), F32), V((2, 4, T, 256), BF16), V((2, 4, T, 256), BF16),
         V((2, 8, 2, 16, 256), BF16), V((2, 8, 2, 16, 256), BF16),
-        dma((11,)), dma((5,)), dma((5,)), dma((7,)), dma((7,)), dma((3, 2, 4)), dma((3, 2, 4)), dma((3, 2)), dma((3, 2)), dma, dma,
+        dma((12,)), dma((5,)), dma((5,)), dma((7,)), dma((7,)), dma((3, 2, 4)), dma((3, 2, 4)), dma((3, 2)), dma((3, 2)), dma, dma,
     ]
     return pl.pallas_call(
         kernel,
@@ -443,7 +453,7 @@
             jax.ShapeDtypeStruct((T, 2048), BF16),
             jax.ShapeDtypeStruct((16, 1024), BF16),
         ),
-        in_specs=[anywhere] * 6 + [vmem, smem, smem, smem, anywhere, anywhere],
+        in_specs=[anywhere] * 7 + [smem, smem, smem, anywhere, anywhere],
         out_specs=(anywhere, vmem),
         scratch_shapes=scratch,
         compiler_params=pltpu.CompilerParams(

time: 87.6 us -> 85.4 us (0.975)
  the two profiles are of different devices: /device:TPU:32 before, /device:TPU:6 now
where the time goes in v4:
time: 85.4 us; the launch traced here: 85.3 us
  Pallas kernels  78.7 us (92%)
  local copies, waits for them, and re-layouts  3.93 us (5%)
  between operations  2.59 us (3%)
    pallas_call x1, Pallas kernels, shards(): pl.pallas_call(kernel, out_shape=(jax.ShapeDtypeStruct((T, 2048), BF16),...  78.7 us
    unnamed x5, local copies, waits for them, and re-layouts  3.93 us

profile of v4, /device:TPU:6, one launch (start us, length us, event | category | flops | bytes accessed | tf_op | source)
XLA Modules:
  0.0 85.3 jit_solution(10839732214891395582)
XLA Ops:
  2.6 1.4 %copy.14.lse_hbm = f32[128,16]{1,0:T(8,128)} copy(f32[128,16]{0,1:T(8,128)} %param.18) | data formatting | bytes 16384 | tf_op args[6]
  4.0 78.7 %attention_backward.1 = (bf16[128,2048]{1,0:T(8,128)(2,1)}, bf16[16,1024]{1,0:T(8,128)(2,1)}) custom-call(bf16[128,4096]{1,0:T(8,128)(2,1)} %x_hbm.1, bf16[128,2048]{1,0:T(8,128)(2,1)} %q_hbm.1, bf16[128,512]{1,0:T(8,128)(2,1)} %k_hbm.1, bf16[128,512]{1,0:T(8,128)(2,1)} %v_hbm.1, bf16[128,2048]{1,0:T(8,128)(2,1)} %o_hbm.1, bf16[128,2048]{1,0:T(8,128)(2,1)} %g_hbm.1, ...), custom_call_target="tpu_custom_call" | custom-call | tf_op jit(solution)/shard_map/attention_backward/pallas_call | solution.py:450
  82.8 0.0 copy-start
  82.8 1.9 %copy.20 = bf16[128,2048]{1,0:T(8,128)(2,1)} copy(bf16[128,2048]{1,0:T(8,128)(2,1)} %get-tuple-element.4) | data formatting | bytes 1048576
  84.6 0.0 copy-done
  84.7 0.6 copy.21
Async XLA Ops:
  82.8 1.9 %copy-start = (bf16[16,1024]{1,0:T(8,128)(2,1)S(1)}, bf16[16,1024]{1,0:T(8,128)(2,1)}, u32[]{:S(2)}) copy-start(bf16[16,1024]{1,0:T(8,128)(2,1)} %get-tuple-element.5) | copy-start | bytes 98308

commit v5 on v4

--- a/solution.py
+++ b/solution.py
@@ -22,6 +22,7 @@
 BL = NT * T
 NB = N_CP // NT
 ORDER = (6, 14, 10, 2, 4, 12, 8, 3, 7, 15, 11, 5, 13, 9, 1)
+HOME = ((6, 14, 10, 2, 7, 15, 11, 3), (4, 12, 8, 5, 13, 9, 1))
 FAR = (4, 3, 5, 2, 6, 1, 7)
 
 
@@ -47,8 +48,8 @@
     qbuf, gbuf, kvbuf_in, stbuf, tagbuf, st_src, tag_src, tags_s, sig_s,
     qs, gs, kvs, kts, st_s, dqt, dkv_s,
     pbuf, xts, xbuf, core_src, core_buf, pair_src, pair_buf, kvbuf,
-    dq_s, dq_src, w_src, w_core, w_own, ysend, ybuf, zsend, zbuf,
-    lsem, asem_s, asem_r, xsem_s, xsem_r, ksem_s, ksem_r, wsem_s, wsem_r, dsem_s, dsem_r,
+    dq_s, dq_src, w_src, w_core, w_own, w_sum, ysend, ybuf, zsend, zbuf,
+    lsem, asem_s, asem_r, xsem_s, xsem_r, ksem_s, ksem_r, wsem_s, wsem_r, dsem_s, dsem_r, ysem_s, ysem_r, zsem_s, zsem_r,
 ):
     r = lax.axis_index("dp")
     c = lax.axis_index("cp")
@@ -355,60 +356,68 @@
         for k in range(4):
             to_other[part, k].wait_recv()
         w_src[part] = tile((1 - q) * 512, part).astype(BF16)
-        w_mates[part] = remote(w_src.at[part], w_core.at[part], wsem_s.at[0, part], wsem_r.at[0, part], r, mate)
+        w_mates[part] = remote(w_src.at[part], w_core.at[part], wsem_s.at[part], wsem_r.at[part], r, mate)
         w_mates[part].start()
 
     def tile_own(part):
         w_own[part] = tile(q * 512, part)
 
-    def send_y(part):
-        w_mates[part].wait_recv()
-        total = w_own[part] + w_core[part].astype(F32)
-        w_own[part] = total
-        ysend[part] = total.astype(BF16)
+    def send_y(part, half):
+        cols = slice(half * DH, (half + 1) * DH)
+        if half == 0:
+            w_mates[part].wait_recv()
+        total = w_own[part, :, :, cols] + w_core[part, :, :, cols].astype(F32)
+        j = 2 * part + half
+        w_sum[j] = total
+        ysend[j] = total.astype(BF16)
         for dl, dy in ((0, 1), (1, 1), (1, 0)):
             yl, yo = (low_y + dl) % 2, (y + dy) % 2
             remote(
-                ysend.at[part, 2 * yl + yo], ybuf.at[part, 2 * low_y + y],
-                wsem_s.at[1, part], wsem_r.at[1, part], z * 2 + yl, x * 4 + yo * 2 + q,
+                ysend.at[j, 2 * yl + yo], ybuf.at[j, 2 * low_y + y],
+                ysem_s.at[j], ysem_r.at[j], z * 2 + yl, x * 4 + yo * 2 + q,
             ).start()
 
-    def send_z(part):
-        take(ybuf.at[part, pl.ds(0, 3)], wsem_r.at[1, part])
-        near = w_own[part, 2 * low_y + y] + ybuf[part, 2 * (1 - low_y) + y].astype(F32)
-        far = ybuf[part, 1 - y].astype(F32) + ybuf[part, 3 - y].astype(F32)
-        zsend[part, :, y] = near.astype(BF16).reshape(8, 16, 256)
-        zsend[part, :, 1 - y] = far.astype(BF16).reshape(8, 16, 256)
+    def send_z(j):
+        take(ybuf.at[j, pl.ds(0, 3)], ysem_r.at[j])
+        near = w_sum[j, 2 * low_y + y] + ybuf[j, 2 * (1 - low_y) + y].astype(F32)
+        far = ybuf[j, 1 - y].astype(F32) + ybuf[j, 3 - y].astype(F32)
+        zsend[j, :, y] = near.astype(BF16).reshape(8, 16, DH)
+        zsend[j, :, 1 - y] = far.astype(BF16).reshape(8, 16, DH)
         for dz in FAR:
             zd = (z + dz) % 8
-            remote(
-                zsend.at[part, zd], zbuf.at[part, z], wsem_s.at[2, part], wsem_r.at[2, part], zd * 2 + low_y, c
-            ).start()
-        zbuf[part, z] = zsend[part, z]
-
-    def finish(part):
-        take(zbuf.at[part, pl.ds(0, 7)], wsem_r.at[2, part])
-        total = zbuf[part, 0].astype(F32)
+            remote(zsend.at[j, zd], zbuf.at[j, z], zsem_s.at[j], zsem_r.at[j], zd * 2 + low_y, c).start()
+        zbuf[j, z] = zsend[j, z]
+
+    def finish(j):
+        take(zbuf.at[j, pl.ds(0, 7)], zsem_r.at[j])
+        total = zbuf[j, 0].astype(F32)
         for i in range(1, 8):
-            total = total + zbuf[part, i].astype(F32)
+            total = total + zbuf[j, i].astype(F32)
         for yy in range(2):
-            start = 512 * (1 - part) + 256 * yy
-            w_out[:, start : start + 256] = total[yy].astype(BF16)
+            start = 512 * (1 - j // 2) + 256 * yy + DH * (j % 2)
+            w_out[:, start : start + DH] = total[yy].astype(BF16)
 
     w_mates = {}
+    for d in HOME[0]:
+        send_dq(d, 0)
     tile_mate(0)
     tile_own(0)
     tile_mate(1)
-    send_y(0)
+    send_y(0, 0)
+    send_y(0, 1)
     tile_own(1)
-    send_y(1)
+    send_y(1, 0)
+    send_y(1, 1)
     send_z(0)
-    lax.fori_loop(1, N_CP, send_dq, 0)
+    for d in HOME[1]:
+        send_dq(d, 0)
     dq_keep = pltpu.make_async_copy(dq_src.at[c], dq_out.at[:, own], lsem.at[2])
     dq_keep.start()
     send_z(1)
-    finish(0)
-    finish(1)
+    send_z(2)
+    send_z(3)
+    for j in range(4):
+        finish(j)
 
     for sends in (to_mate, to_pair, to_other):
         for send in sends.values():
@@ -422,8 +431,9 @@
         send.wait_send()
     for part in range(2):
         w_mates[part].wait_send()
-        take(ybuf.at[part, pl.ds(0, 3)], wsem_s.at[1, part])
-        take(zbuf.at[part, pl.ds(0, 7)], wsem_s.at[2, part])
+    for j in range(4):
+        take(ybuf.at[j, pl.ds(0, 3)], ysem_s.at[j])
+        take(zbuf.at[j, pl.ds(0, 7)], zsem_s.at[j])
 
 
 def shards(layer_input, queries, keys, values, outputs, out_grad, log_sum_exp, group_first, span_index, seq_length):
@@ -443,9 +453,10 @@
         V((NB * NB, BL, BL), F32), V((4, 1024, T), BF16), V((1024, 1024), BF16), V((2, 1024, DH), BF16),
         V((2, 1024, DH), BF16), V((2, 1024, DH), BF16), V((2, 1024, DH), BF16), V((2, 1024, 256), BF16),
         V((16, T, DH), BF16), V((16, T, DH), BF16), V((2, 4, T, 256), BF16), V((2, 4, T, 256), BF16),
-        V((2, 4, T, 256), F32), V((2, 4, T, 256), BF16), V((2, 4, T, 256), BF16),
-        V((2, 8, 2, 16, 256), BF16), V((2, 8, 2, 16, 256), BF16),
-        dma((12,)), dma((5,)), dma((5,)), dma((7,)), dma((7,)), dma((3, 2, 4)), dma((3, 2, 4)), dma((3, 2)), dma((3, 2)), dma, dma,
+        V((2, 4, T, 256), F32), V((4, 4, T, DH), F32), V((4, 4, T, DH), BF16), V((4, 4, T, DH), BF16),
+        V((4, 8, 2, 16, DH), BF16), V((4, 8, 2, 16, DH), BF16),
+        dma((12,)), dma((5,)), dma((5,)), dma((7,)), dma((7,)), dma((3, 2, 4)), dma((3, 2, 4)), dma((2,)), dma((2,)), dma, dma,
+        dma((4,)), dma((4,)), dma((4,)), dma((4,)),
     ]
     return pl.pallas_call(
         kernel,

time: 85.4 us -> 84.7 us (level)
  the two profiles are of different devices: /device:TPU:6 before, /device:TPU:1 now
where the time goes in v5:
time: 84.7 us; the launch traced here: 84.5 us
  Pallas kernels  78 us (92%)
  local copies, waits for them, and re-layouts  3.93 us (5%)
  between operations  2.59 us (3%)
    pallas_call x1, Pallas kernels, shards(): pl.pallas_call(kernel, out_shape=(jax.ShapeDtypeStruct((T, 2048), BF16),...  78 us
    unnamed x5, local copies, waits for them, and re-layouts  3.93 us

profile of v5, /device:TPU:1, one launch (start us, length us, event | category | flops | bytes accessed | tf_op | source)
XLA Modules:
  0.0 84.5 jit_solution(7588639931387685810)
XLA Ops:
  2.6 1.4 %copy.14.lse_hbm = f32[128,16]{1,0:T(8,128)} copy(f32[128,16]{0,1:T(8,128)} %param.18) | data formatting | bytes 16384 | tf_op args[6]
  4.0 78.0 %attention_backward.1 = (bf16[128,2048]{1,0:T(8,128)(2,1)}, bf16[16,1024]{1,0:T(8,128)(2,1)}) custom-call(bf16[128,4096]{1,0:T(8,128)(2,1)} %x_hbm.1, bf16[128,2048]{1,0:T(8,128)(2,1)} %q_hbm.1, bf16[128,512]{1,0:T(8,128)(2,1)} %k_hbm.1, bf16[128,512]{1,0:T(8,128)(2,1)} %v_hbm.1, bf16[128,2048]{1,0:T(8,128)(2,1)} %o_hbm.1, bf16[128,2048]{1,0:T(8,128)(2,1)} %g_hbm.1, ...), custom_call_target="tpu_custom_call" | custom-call | tf_op jit(solution)/shard_map/attention_backward/pallas_call | solution.py:461
  82.0 0.0 copy-start
  82.0 1.9 %copy.20 = bf16[128,2048]{1,0:T(8,128)(2,1)} copy(bf16[128,2048]{1,0:T(8,128)(2,1)} %get-tuple-element.4) | data formatting | bytes 1048576
  83.9 0.0 copy-done
  83.9 0.6 copy.21
Async XLA Ops:
  82.0 1.9 %copy-start = (bf16[16,1024]{1,0:T(8,128)(2,1)S(1)}, bf16[16,1024]{1,0:T(8,128)(2,1)}, u32[]{:S(2)}) copy-start(bf16[16,1024]{1,0:T(8,128)(2,1)} %get-tuple-element.5) | copy-start | bytes 98308

commit v6 on v5

--- a/solution.py
+++ b/solution.py
@@ -333,12 +333,14 @@
     share(0)
     sum_pair(1)
     hand_on(2)
-    share(1)
 
     for p in range(N_CP):
         dq_s[p] = (dqt[p // NT, :, (p % NT) * T : (p % NT + 1) * T] * SCALE).T.astype(BF16)
     for m in range(N_CP):
         dq_src[m] = dq_s[place[m]]
+
+    share(1)
+
 
     def send_dq(d, _):
         xd, yd, qd, cd = row_peer(d)

time: 84.7 us -> 84.7 us (level)
  no operation moved by 1% of the time
where the time goes in v6:
time: 84.7 us; the launch traced here: 84.5 us
  Pallas kernels  78 us (92%)
  local copies, waits for them, and re-layouts  3.93 us (5%)
  between operations  2.59 us (3%)
    pallas_call x1, Pallas kernels, shards(): pl.pallas_call(kernel, out_shape=(jax.ShapeDtypeStruct((T, 2048), BF16),...  78 us
    unnamed x5, local copies, waits for them, and re-layouts  3.93 us

profile of v6, /device:TPU:1, one launch (start us, length us, event | category | flops | bytes accessed | tf_op | source)
XLA Modules:
  0.0 84.5 jit_solution(18124435834358519709)
XLA Ops:
  2.6 1.4 %copy.14.lse_hbm = f32[128,16]{1,0:T(8,128)} copy(f32[128,16]{0,1:T(8,128)} %param.18) | data formatting | bytes 16384 | tf_op args[6]
  4.0 78.0 %attention_backward.1 = (bf16[128,2048]{1,0:T(8,128)(2,1)}, bf16[16,1024]{1,0:T(8,128)(2,1)}) custom-call(bf16[128,4096]{1,0:T(8,128)(2,1)} %x_hbm.1, bf16[128,2048]{1,0:T(8,128)(2,1)} %q_hbm.1, bf16[128,512]{1,0:T(8,128)(2,1)} %k_hbm.1, bf16[128,512]{1,0:T(8,128)(2,1)} %v_hbm.1, bf16[128,2048]{1,0:T(8,128)(2,1)} %o_hbm.1, bf16[128,2048]{1,0:T(8,128)(2,1)} %g_hbm.1, ...), custom_call_target="tpu_custom_call" | custom-call | tf_op jit(solution)/shard_map/attention_backward/pallas_call | solution.py:463
  82.0 0.0 copy-start
  82.0 1.9 %copy.20 = bf16[128,2048]{1,0:T(8,128)(2,1)} copy(bf16[128,2048]{1,0:T(8,128)(2,1)} %get-tuple-element.4) | data formatting | bytes 1048576
  83.9 0.0 copy-done
  83.9 0.6 copy.21
Async XLA Ops:
  82.0 1.9 %copy-start = (bf16[16,1024]{1,0:T(8,128)(2,1)S(1)}, bf16[16,1024]{1,0:T(8,128)(2,1)}, u32[]{:S(2)}) copy-start(bf16[16,1024]{1,0:T(8,128)(2,1)} %get-tuple-element.5) | copy-start | bytes 98308
